TPU v7x, 256 devices: a whole 4x4x8 slice. The times are simulated.
256 devices in a mesh: dp: 8 (over y, core), batch: 32 (over z, x).
Axes of the slice: x: 4, y: 4, z: 8, core: 2. Of those that a mesh axis runs over, the one named last changes fastest.
Arguments:
- waveform: float32 [2048, 512], P(('dp', 'batch')), may hold values from -6 to 6
- lengths: int32 [2048], P(('dp', 'batch')), may hold values from 256 to 512
- destination: int32 [2048], P(('dp', 'batch')), may hold values from 0 to 31, as said below
- tokens: int32 [2048], P(('dp', 'batch')), may hold values from 1 to 32
- cotangent: bfloat16 [2048, 24, 512], P(('dp', 'batch')), may hold values from -6000 to 6000
- initial_filter_weight: bfloat16 [512, 10], P('dp'), may hold values from -2 to 2
- middle_filter_weight: bfloat16 [512, 1536], P('dp'), may hold values from -0.15625 to 0.15625
- final_filter_weight: bfloat16 [512, 1536], P('dp'), may hold values from -0.15625 to 0.15625
Outputs:
- grad_first: float32 [512, 10], P('dp')
- grad_second: float32 [512, 1536], P('dp')
- grad_third: float32 [512, 1536], P('dp')
- grad_rms: float32 [1], replicated
Inputs may be any that keep to these rules, and one draw needn't show every extreme that they name: `destination`: every device receives exactly 8 segments from the devices of its dp row; at most 2 segments go from one device to one device, and every device sends exactly 2 to some device.
All inputs are finite; a program needn't handle non-finite values.
Results may differ from a plain program's by a relative error of at most 0.0063.
Values may be sent and summed in bfloat16 or wider, within the bound.
A program may use at most 64 MiB of HBM per device.

v0:
```python
import jax
import jax.numpy as jnp
from jax import lax
from jax.sharding import PartitionSpec as P


def out_length(amount, kernel, stride):
    return (amount - kernel) // stride + 1


def layer_norm(hidden):
    average = jnp.mean(hidden, axis=-1, keepdims=True)
    centred = hidden - average
    variance = jnp.mean(centred * centred, axis=-1, keepdims=True)
    inverse = lax.rsqrt(variance + 1e-05)
    return (centred * inverse, inverse)


def norm_back(grad_out, normed, inverse):
    first_mean = jnp.mean(grad_out, axis=-1, keepdims=True)
    second_mean = jnp.mean(grad_out * normed, axis=-1, keepdims=True)
    return inverse * (grad_out - first_mean - normed * second_mean)


def gelu_slope(normed):
    return (
        0.5 * (1.0 + lax.erf(normed * 0.7071067811865476))
        + normed * jnp.exp(-0.5 * normed * normed) * 0.3989422804014327
    )


def strided_taps(values, frames):
    return jnp.concatenate(
        [values[:, tap_index : tap_index + 2 * (frames - 1) + 1 : 2] for tap_index in range(3)],
        axis=-1,
    )


def spread_back(patch_delta, frames_in, chan_width):
    first_tap = patch_delta[..., :chan_width]
    middle_tap = patch_delta[..., chan_width : 2 * chan_width]
    last_tap = patch_delta[..., 2 * chan_width :]
    even_rows = jnp.pad(first_tap, ((0, 0), (0, 1), (0, 0))) + jnp.pad(
        last_tap, ((0, 0), (1, 0), (0, 0))
    )
    odd_rows = jnp.pad(middle_tap, ((0, 0), (0, 1), (0, 0)))
    merged = jnp.stack([even_rows, odd_rows], axis=2)
    return merged.reshape(merged.shape[0], -1, chan_width)[:, :frames_in]


def segment_gradient_list(
    waveform, lengths, token_weight, cotangent, first_weight, second_weight, third_weight
):
    seg_count, samples = waveform.shape
    chan_width = second_weight.shape[0]
    position = jnp.arange(samples, dtype=jnp.int32)
    inside = (position[None, :] < lengths[:, None]).astype(jnp.float32)
    length_float = lengths.astype(jnp.float32)[:, None]
    average = jnp.sum(waveform * inside, axis=1, keepdims=True) / length_float
    centred = (waveform - average) * inside
    variance = jnp.sum(centred * centred, axis=1, keepdims=True) / length_float
    normal_wave = centred * lax.rsqrt(variance + 1e-07)
    frames0 = out_length(samples, 10, 5)
    frames1 = out_length(frames0, 3, 2)
    frames2 = out_length(frames1, 3, 2)
    patches0 = jnp.stack(
        [
            normal_wave[:, tap_index : tap_index + 5 * (frames0 - 1) + 1 : 5]
            for tap_index in range(10)
        ],
        axis=-1,
    )
    hidden0 = jnp.einsum(
        "sfk,ck->sfc", patches0, first_weight.astype(jnp.float32), precision=lax.Precision.HIGHEST
    )
    normed0, inverse0 = layer_norm(hidden0)
    active0 = jax.nn.gelu(normed0, approximate=False).astype(jnp.bfloat16)
    patches1 = strided_taps(active0, frames1).reshape(seg_count * frames1, 3 * chan_width)
    hidden1 = jnp.dot(patches1, second_weight.T, preferred_element_type=jnp.float32).reshape(
        seg_count, frames1, chan_width
    )
    normed1, inverse1 = layer_norm(hidden1)
    active1 = jax.nn.gelu(normed1, approximate=False).astype(jnp.bfloat16)
    patches2 = strided_taps(active1, frames2).reshape(seg_count * frames2, 3 * chan_width)
    hidden2 = jnp.dot(patches2, third_weight.T, preferred_element_type=jnp.float32).reshape(
        seg_count, frames2, chan_width
    )
    normed2, inverse2 = layer_norm(hidden2)
    valid_two = out_length(out_length(out_length(lengths, 10, 5), 3, 2), 3, 2)
    frame_weight = (jnp.arange(frames2, dtype=jnp.int32)[None, :] < valid_two[:, None]).astype(
        jnp.float32
    ) * token_weight[:, None]
    upward2 = cotangent.astype(jnp.float32) * frame_weight[:, :, None] * gelu_slope(normed2)
    delta_two = (
        norm_back(upward2, normed2, inverse2)
        .astype(jnp.bfloat16)
        .reshape(seg_count * frames2, chan_width)
    )
    grad_third = jnp.dot(delta_two.T, patches2, preferred_element_type=jnp.float32)
    patch_delta2 = jnp.dot(delta_two, third_weight, preferred_element_type=jnp.float32).reshape(
        seg_count, frames2, 3 * chan_width
    )
    upward1 = spread_back(patch_delta2, frames1, chan_width) * gelu_slope(normed1)
    delta_one = (
        norm_back(upward1, normed1, inverse1)
        .astype(jnp.bfloat16)
        .reshape(seg_count * frames1, chan_width)
    )
    grad_second = jnp.dot(delta_one.T, patches1, preferred_element_type=jnp.float32)
    patch_delta1 = jnp.dot(delta_one, second_weight, preferred_element_type=jnp.float32).reshape(
        seg_count, frames1, 3 * chan_width
    )
    upward0 = spread_back(patch_delta1, frames0, chan_width) * gelu_slope(normed0)
    delta_zero = norm_back(upward0, normed0, inverse0)
    grad_first = jnp.einsum("sfc,sfk->ck", delta_zero, patches0, precision=lax.Precision.HIGHEST)
    return (grad_first, grad_second, grad_third)


def squares_of(pieces):
    return (
        jnp.sum(pieces[0] * pieces[0])
        + jnp.sum(pieces[1] * pieces[1])
        + jnp.sum(pieces[2] * pieces[2])
    )


def local(
    waveform,
    lengths,
    destination,
    tokens,
    cotangent,
    initial_filter_weight,
    middle_filter_weight,
    final_filter_weight,
):
    batch_size = lax.axis_size("batch")
    seg_count, samples = waveform.shape
    capacity = max(2, 2 * seg_count // batch_size)
    slot_total = batch_size * capacity
    order = jnp.arange(seg_count, dtype=jnp.int32)
    matching = destination[:, None] == destination[None, :]
    earlier = order[None, :] < order[:, None]
    ranking = jnp.sum(jnp.logical_and(matching, earlier), axis=1)
    slot_index = destination * capacity + ranking
    placing = (jnp.arange(slot_total, dtype=jnp.int32)[:, None] == slot_index[None, :]).astype(
        jnp.float32
    )
    details = jnp.stack(
        [
            lengths.astype(jnp.float32),
            tokens.astype(jnp.float32),
            jnp.ones((seg_count,), jnp.float32),
        ],
        axis=1,
    )
    send_wave = jnp.dot(placing, waveform, precision=lax.Precision.HIGHEST)
    send_detail = jnp.dot(placing, details, precision=lax.Precision.HIGHEST)
    token_part = jnp.sum(tokens.astype(jnp.float32))
    token_sum = lax.psum(token_part, ("dp", "batch"))
    got_wave, got_detail = (
        lax.all_to_all(send_wave, "batch", split_axis=0, concat_axis=0, tiled=True),
        lax.all_to_all(send_detail, "batch", split_axis=0, concat_axis=0, tiled=True),
    )
    filled = got_detail[:, 2]
    before = jnp.cumsum(filled) - filled
    picking = jnp.logical_and(
        before[None, :] == order[:, None].astype(jnp.float32), filled[None, :] > 0.5
    ).astype(jnp.float32)
    local_wave = jnp.dot(picking, got_wave, precision=lax.Precision.HIGHEST)
    local_detail = jnp.dot(picking, got_detail, precision=lax.Precision.HIGHEST)
    local_lengths = local_detail[:, 0].astype(jnp.int32)
    local_tokens = local_detail[:, 1]
    first_full, second_full, third_full = (
        lax.all_gather(initial_filter_weight, "dp", axis=0, tiled=True),
        lax.all_gather(middle_filter_weight, "dp", axis=0, tiled=True),
        lax.all_gather(final_filter_weight, "dp", axis=0, tiled=True),
    )
    chan_width = second_full.shape[0]
    block_size = min(16, seg_count)
    block_count = seg_count // block_size
    frames_last = cotangent.shape[1]

    def accumulate(running_total, pieces):
        waveform_block, length_slice_block, token_slice_block, cotangent_block = pieces
        summand_terms = segment_gradient_list(
            waveform_block,
            length_slice_block,
            token_slice_block,
            cotangent_block,
            first_full,
            second_full,
            third_full,
        )
        return (
            (
                running_total[0] + summand_terms[0],
                running_total[1] + summand_terms[1],
                running_total[2] + summand_terms[2],
            ),
            None,
        )

    start = (
        jnp.zeros((chan_width, 10), jnp.float32),
        jnp.zeros((chan_width, 3 * chan_width), jnp.float32),
        jnp.zeros((chan_width, 3 * chan_width), jnp.float32),
    )
    sums, unused = lax.scan(
        accumulate,
        start,
        (
            local_wave.reshape(block_count, block_size, samples),
            local_lengths.reshape(block_count, block_size),
            local_tokens.reshape(block_count, block_size),
            cotangent.reshape(block_count, block_size, frames_last, chan_width),
        ),
    )
    owner_part = (
        lax.psum_scatter(sums[0], "dp", scatter_dimension=0, tiled=True),
        lax.psum_scatter(sums[1], "dp", scatter_dimension=0, tiled=True),
        lax.psum_scatter(sums[2], "dp", scatter_dimension=0, tiled=True),
    )
    owned = lax.psum((owner_part[0], owner_part[1], owner_part[2]), "batch")
    square_part = squares_of(owned) * (1.0 / batch_size)
    square_sum = lax.psum(square_part, ("dp", "batch"))
    scaled_first = owned[0] / token_sum
    scaled_second = owned[1] / token_sum
    scaled_third = owned[2] / token_sum
    param_count = chan_width * 10 + 6 * chan_width * chan_width
    rms_value = jnp.sqrt(square_sum / param_count) / token_sum
    factor = 1.0 / jnp.maximum(rms_value, 1.0)
    return (
        scaled_first * factor,
        scaled_second * factor,
        scaled_third * factor,
        jnp.reshape(rms_value, (1,)),
    )


def solution(mesh):
    placed = (
        P(("dp", "batch"), None),
        P(("dp", "batch")),
        P(("dp", "batch")),
        P(("dp", "batch")),
        P(("dp", "batch"), None, None),
        P("dp", None),
        P("dp", None),
        P("dp", None),
    )
    return jax.shard_map(
        local,
        mesh=mesh,
        in_specs=placed,
        out_specs=(P("dp", None), P("dp", None), P("dp", None), P()),
        check_vma=False,
    )
```

profile of v0, /device:TPU:1, one launch (start us, length us, event | category | flops | bytes accessed | tf_op | source)
XLA Modules:
  0.0 446.4 jit_solution(16447220614461798637)
XLA Ops:
  11.1 11.9 %all-to-all-start = ((f32[32,2,3]{2,1,0:T(2,128)}), f32[32,2,3]{2,1,0:T(2,128)S(1)}, u32[]{:S(2)}, u32[]{:S(2)}) async-start(f32[32,2,3]{2,1,0:T(2,128)} %bitcast.2), calls=%async_computation | async-start | bytes 65536 | tf_op jit(solution)/shard_map/all_to_all | solution.py:163
  23.9 14.2 %all-gather = bf16[8,64,10]{1,2,0:T(8,128)(2,1)S(1)} all-gather(bf16[1,64,10]{1,2,0:T(8,128)(2,1)} %bitcast.95), channel_id=1, replica_groups=mesh['dp'=8,'batch'=32] {'dp'}, dimensions={0}, use_global_device_ids=true | all-gather | bytes 11520 | tf_op jit(solution)/shard_map/all_gather | solution.py:175
  39.0 9.5 %all-to-all-start.1 = ((f32[32,2,512]{2,1,0:T(2,128)}), f32[32,2,512]{2,1,0:T(2,128)S(1)}, u32[]{:S(2)}, u32[]{:S(2)}) async-start(f32[32,2,512]{2,1,0:T(2,128)} %all_to_all.19), calls=%async_computation.1 | async-start | bytes 262144 | tf_op jit(solution)/shard_map/all_to_all | solution.py:162
  49.3 8.9 %all-to-all-done.1 = f32[32,2,512]{2,1,0:T(2,128)S(1)} async-done(((f32[32,2,512]{2,1,0:T(2,128)}), f32[32,2,512]{2,1,0:T(2,128)S(1)}, u32[]{:S(2)}, u32[]{:S(2)}) %all-to-all-start.1) | async-done | bytes 131104 | tf_op jit(solution)/shard_map/all_to_all | solution.py:162
  63.3 4.1 fusion.2
  68.6 2.9 slice.115
  72.1 2.5 fusion.93
  75.8 2.3 fusion.33
  78.2 1.5 slice.120
  82.6 2.5 fusion.94
  90.2 2.7 convolution_bitcast_fusion
  94.1 2.3 convolution_bitcast_fusion.1
  96.5 2.3 fusion.24
  101.3 1.9 fusion.84
  103.2 4.6 %fusion.28 = f32[512,10]{1,0:T(8,128)} fusion(f32[8,101,512]{2,1,0:T(8,128)S(1)} %get-tuple-element.47, f32[8,101,512]{2,1,0:T(8,128)S(1)} %get-tuple-element.61, f32[8,101]{1,0:T(8,128)S(1)} %broadcast_multiply_fusion.6, f32[8,101]{1,0:T(8,128)S(1)} %broadcast_multiply_fusion.7, f32[8,101]{1,0:T(8,128)S(1)} %copy-done.19, f32[8,101]{1,0:T(8,128)S(1)} %copy-done.15, ...), kind=kOutput, calls=%fused_computation.47 | convolution fusion | flops 52125696 | bytes 3375296 | tf_op jit(solution)/shard_map/while/body/eval_jaxpr/sfc,sfk->ck/dot_general | solution.py:115
  107.9 16.2 %reduce-scatter.6.cloned.1.call-done = f32[64,1536]{1,0:T(8,128)} async-done(((f32[512,1536]{1,0:T(8,128)}), f32[64,1536]{1,0:T(8,128)}) %reduce-scatter.6.cloned.1.call-update) | async-done | bytes 393232 | tf_op jit(solution)/shard_map/reduce_scatter | solution.py:221
  124.1 39.5 %reduce-scatter.8.cloned.1.call-done = f32[64,1536]{1,0:T(8,128)} async-done(((f32[512,1536]{1,0:T(8,128)}), f32[64,1536]{1,0:T(8,128)}) %reduce-scatter.8.cloned.1.call-update) | async-done | bytes 393232 | tf_op jit(solution)/shard_map/reduce_scatter | solution.py:222
  164.3 34.6 %reduce-scatter.10.cloned.1.call-done = f32[64,10]{1,0:T(8,128)} async-done(((f32[512,10]{1,0:T(8,128)}), f32[64,10]{1,0:T(8,128)}) %reduce-scatter.10.cloned.1.call-update) | async-done | bytes 2576
  199.7 61.9 %psum.35 = f32[64,10]{0,1:T(8,128)S(1)} all-reduce(f32[64,10]{0,1:T(8,128)S(1)} %copy.44), channel_id=1, replica_groups=mesh['dp'=8,'batch'=32] {'batch'}, use_global_device_ids=true, to_apply=%region_17.18 | all-reduce | flops 640 | bytes 5120 | tf_op jit(solution)/shard_map/psum | solution.py:224
  262.1 85.4 %all-reduce.10.cloned.1.call-done = (f32[64,1536]{1,0:T(8,128)}, f32[64,1536]{1,0:T(8,128)}) async-done(((f32[64,1536]{1,0:T(8,128)}, f32[64,1536]{1,0:T(8,128)}), (f32[64,1536]{1,0:T(8,128)}, f32[64,1536]{1,0:T(8,128)})) %all-reduce.10.cloned.1.call-update) | async-done | bytes 786448 | tf_op jit(solution)/shard_map/psum | solution.py:224
  347.6 1.8 multiply_reduce_fusion.5
  349.3 1.7 multiply_reduce_fusion.4
  353.0 79.0 %all-reduce.6 = (f32[]{:T(128)}, f32[]{:T(128)}) all-reduce(f32[]{:T(128)S(6)} %mul.368, f32[]{:T(128)} %convert_reduce_fusion.1), channel_id=1, replica_groups=mesh['dp'=8,'batch'=32] {'dp','batch'}, use_global_device_ids=true, to_apply=%region_27.28 | all-reduce | flops 2 | bytes 16 | tf_op jit(solution)/shard_map/psum | solution.py:226
  434.6 2.4 divide_multiply_fusion.1
  (148 shorter events, 30.6 us)
Async XLA Ops:
  7.2 16.5 %copy-start = (f32[8,512]{1,0:T(8,128)S(1)}, f32[8,512]{1,0:T(8,128)}, u32[]{:S(2)}) copy-start(f32[8,512]{1,0:T(8,128)} %param.8) | copy-start | bytes 49156
  7.2 64.9 %all-gather.4.cloned.1.call-start = ((), (), s32[]{:S(2)}) async-start(), calls=%async_computation.5 | async-start | bytes 1769472 | tf_op jit(solution)/shard_map/all_gather | solution.py:176
  11.1 27.9 %all-to-all-start = ((f32[32,2,3]{2,1,0:T(2,128)}), f32[32,2,3]{2,1,0:T(2,128)S(1)}, u32[]{:S(2)}, u32[]{:S(2)}) async-start(f32[32,2,3]{2,1,0:T(2,128)} %bitcast.2), calls=%async_computation | async-start | bytes 65536 | tf_op jit(solution)/shard_map/all_to_all | solution.py:163
  22.9 59.6 %all-gather.6.cloned.1.call-start = ((), (), s32[]{:S(2)}) async-start(), calls=%async_computation.6 | async-start | bytes 1769472 | tf_op jit(solution)/shard_map/all_gather | solution.py:177
  39.0 19.3 %all-to-all-start.1 = ((f32[32,2,512]{2,1,0:T(2,128)}), f32[32,2,512]{2,1,0:T(2,128)S(1)}, u32[]{:S(2)}, u32[]{:S(2)}) async-start(f32[32,2,512]{2,1,0:T(2,128)} %all_to_all.19), calls=%async_computation.1 | async-start | bytes 262144 | tf_op jit(solution)/shard_map/all_to_all | solution.py:162
  48.5 75.6 %reduce-scatter.6.cloned.1.call-start = ((), (), s32[]{:S(2)}) async-start(), calls=%async_computation.7 | async-start | bytes 3538944 | tf_op jit(solution)/shard_map/reduce_scatter | solution.py:221
  68.6 6.1 %copy-start.1 = (bf16[8,50,512]{2,1,0:T(8,128)(2,1)}, bf16[8,50,512]{2,1,0:T(8,128)(2,1)S(1)}, u32[]{:S(2)}) copy-start(bf16[8,50,512]{2,1,0:T(8,128)(2,1)S(1)} %slice.116) | copy-start | bytes 1228804
  82.6 2.7 copy-start.13
  82.6 2.7 copy-start.22
  85.1 1.4 copy-start.4
  87.3 0.7 copy-start.21
  89.1 1.0 copy-start.2
  89.1 1.2 copy-start.3
  92.9 0.9 copy-start.7
  92.9 1.0 copy-start.10
  92.9 1.1 copy-start.11
  92.9 1.2 copy-start.12
  92.9 70.7 %reduce-scatter.8.cloned.1.call-start = ((), (), s32[]{:S(2)}) async-start(), calls=%async_computation.8 | async-start | bytes 3538944 | tf_op jit(solution)/shard_map/reduce_scatter | solution.py:222
  96.4 102.4 %reduce-scatter.10.cloned.1.call-start = ((), (), s32[]{:S(2)}) async-start(), calls=%async_computation.9 | async-start | bytes 294912
  100.6 0.7 copy-start.19
  101.3 1.9 copy-start.9
  103.2 60.4 %copy-start.23 = (s32[8]{0:T(128)S(1)}, s32[8]{0:T(128)}, u32[]{:S(2)}) copy-start(s32[8]{0:T(128)} %param.11) | copy-start | bytes 100
  107.8 239.7 %all-reduce.10.cloned.1.call-start = ((), (), s32[]{:S(2)}) async-start(), calls=%async_computation.10 | async-start | bytes 1572864 | tf_op jit(solution)/shard_map/psum | solution.py:224
  347.6 89.5 %copy-start.5 = (f32[64,1536]{1,0:T(8,128)S(1)}, f32[64,1536]{1,0:T(8,128)}, u32[]{:S(2)}) copy-start(f32[64,1536]{1,0:T(8,128)} %get-tuple-element.46) | copy-start | bytes 1179652
  (8 other events, 5.0 us)
Sparse Core Ops, SparseCore 0:
  9.8 31.3 all-gather.3
  43.1 27.3 all-gather.5
  93.1 30.9 reduce-scatter.5
  126.5 37.0 reduce-scatter.7
  166.5 32.2 reduce-scatter.9
  202.4 145.0 all-reduce.9
where the time goes:
time: 447 us; the launch traced here: 446 us
  waiting for transfers between devices  186 us (42%)
  blocking collectives  155 us (35%)
  other arithmetic  25.2 us (6%)
  starting transfers between devices  21.8 us (5%)
  matrix products  19.9 us (4%)
  between operations  19.2 us (4%)
  local copies, waits for them, and re-layouts  19.1 us (4%)
    psum x1, waiting for transfers between devices, local(): owned = lax.psum((owner_part[0], owner_part[1], owner_part[2]), 'batch')  85.4 us
    psum x1, blocking collectives, local(): square_sum = lax.psum(square_part, ('dp', 'batch'))  79 us
    psum x1, blocking collectives, local(): owned = lax.psum((owner_part[0], owner_part[1], owner_part[2]), 'batch')  61.9 us
    reduce_scatter x1, waiting for transfers between devices, local(): lax.psum_scatter(sums[2], 'dp', scatter_dimension=0, tiled=True)  39.5 us
    unnamed x7, waiting for transfers between devices  36 us
    reduce_scatter x1, waiting for transfers between devices, local(): lax.psum_scatter(sums[1], 'dp', scatter_dimension=0, tiled=True)  16.2 us
    all_gather x1, blocking collectives, local(): lax.all_gather(initial_filter_weight, 'dp', axis=0, tiled=True)  14.2 us
    all_to_all x1, starting transfers between devices, local(): lax.all_to_all(send_detail, 'batch', split_axis=0, concat_axis=0, tiled=T...  11.9 us
  transfers between devices with their start and end apart: 8, of which 5 were waited for; matrix products, arithmetic and copies ran while one was open for 9% of the time, Pallas kernels for 0%

commit v1 on v0

v1 whole, which is shorter than its diff:
```python
import functools

import jax
import jax.numpy as jnp
from jax import lax
from jax.experimental import pallas as pl
from jax.experimental.pallas import tpu as pltpu
from jax.sharding import PartitionSpec as P

F32 = jnp.float32
BF16 = jnp.bfloat16
D = 512
SEG = 8
J = 26
ROWS = J * SEG
F2 = 24
ROWS2 = F2 * SEG
NT = (((1,), (1,)), ((), ()))
TN = (((0,), (0,)), ((), ()))
NN = (((1,), (0,)), ((), ()))


def mm(a, b, dims):
    return lax.dot_general(a, b, dims, preferred_element_type=F32)


def iota(shape, dim):
    return lax.broadcasted_iota(jnp.int32, shape, dim)


def mean(x):
    return jnp.sum(x, axis=-1, keepdims=True) * (1.0 / D)


def norm_gelu(hidden):
    centred = hidden - mean(hidden)
    inverse = lax.rsqrt(mean(centred * centred) + 1e-05)
    normed = centred * inverse
    cdf = 0.5 + 0.5 * lax.erf(normed * 0.7071067811865476)
    slope = cdf + normed * jnp.exp(-0.5 * normed * normed) * 0.3989422804014327
    return normed, inverse, normed * cdf, slope


def norm_back(grad, normed, inverse):
    return inverse * (grad - mean(grad) - normed * mean(grad * normed))


def pick_waves(got):
    lane_pick = (iota((SEG, 128), 1) == 127).astype(BF16)
    token_row = mm(lane_pick, got, NT)
    column = iota((SEG, 512), 1)
    carries = jnp.logical_and(column % 16 >= 8, column % 4 == 3)
    filled = jnp.where(jnp.logical_and(carries, token_row > 0.5), 1.0, 0.0).astype(BF16)
    row_slot = iota((512, 512), 0)
    row_slot = (row_slot // 16) * 2 + (row_slot // 4) % 2
    column_slot = iota((512, 512), 1)
    column_slot = (column_slot // 16) * 2 + (column_slot // 4) % 2
    weight = jnp.where(row_slot < column_slot, 1.0, 0.0) + jnp.where(
        row_slot == column_slot, 64.0, 0.0
    )
    place = mm(filled, weight.astype(BF16), NN) - 64.0
    target = place + ((column // 8) % 2 * 32 + (column % 4) * 8).astype(F32)
    target = jnp.where(place > -0.5, target, -1.0)
    picking = jnp.where(iota((64, 512), 0).astype(F32) == target[0:1], 1.0, 0.0).astype(BF16)
    picked = mm(picking, got, NN)
    last = picked[56:64]
    length = last[:, 126:127] + 256.0
    tokens = last[:, 127:128]
    low_last = jnp.where(iota((SEG, 128), 1) < 126, last, 0.0)
    pieces = [picked[8 * i : 8 * i + 8] + picked[32 + 8 * i : 40 + 8 * i] for i in range(3)]
    pieces.append(picked[24:32] + low_last)
    return jnp.concatenate(pieces, axis=1), length, tokens


def first_taps(wave, length):
    inside = iota((SEG, D), 1).astype(F32) < length
    average = jnp.sum(jnp.where(inside, wave, 0.0), axis=1, keepdims=True) / length
    centred = jnp.where(inside, wave - average, 0.0)
    variance = jnp.sum(centred * centred, axis=1, keepdims=True) / length
    normal = centred * lax.rsqrt(variance + 1e-07)
    padded = jnp.concatenate([normal, jnp.zeros((SEG, 256), F32)], axis=1)
    rows = []
    for j in range(J):
        tile, shift = (20 * j) // 128, (20 * j) % 128
        pair = padded[:, tile * 128 : tile * 128 + 256]
        if shift:
            pair = pltpu.roll(pair, 256 - shift, axis=1)
        rows.append(pair[:, :128])
    taps = jnp.concatenate(rows, axis=0)
    return jnp.where(iota((ROWS, 128), 1) < 32, taps, 0.0)


def forward_first(got, w0_ref, r):
    wave, length, tokens = pick_waves(got)
    taps = first_taps(wave, length)
    high = taps.astype(BF16).astype(F32)
    both = high + pltpu.roll(taps - high, 32, axis=1)
    both_narrow = both.astype(BF16)
    narrow_lane = iota((ROWS, 128), 1)
    for c in range(4):
        moved = pltpu.roll(both, 128 - 5 * c, axis=1) if c else both
        keep = narrow_lane % 32 < 10
        moved = jnp.where(jnp.logical_and(keep, narrow_lane < 64), moved, 0.0)
        r["x4"][c * ROWS : (c + 1) * ROWS] = moved.astype(BF16)
    w0 = w0_ref[...]
    tap_row, tap_column = iota((128, 128), 0), iota((128, 128), 1)
    for c in range(4):
        placing = jnp.logical_and(tap_row % 32 == tap_column + 5 * c, tap_row < 64)
        placing = jnp.logical_and(placing, tap_column < 10)
        weight = mm(jnp.where(placing, 1.0, 0.0).astype(BF16), w0, NT).astype(BF16)
        r["z0"][c * ROWS : (c + 1) * ROWS] = mm(both_narrow, weight, NN)
    l2 = ((((length - 10.0) * 0.2).astype(jnp.int32) + 1 - 3) // 2 + 1 - 3) // 2 + 1
    r["info"][0:8] = jnp.broadcast_to(l2.astype(F32), (SEG, 128))
    r["info"][8:16] = jnp.broadcast_to(tokens, (SEG, 128))

    for c in range(4):

        def body(m, carry, c=c):
            at = pl.multiple_of(m * 16, 16)
            rows = pl.ds(pl.multiple_of(c * ROWS + m * 16, 16), 16)
            here = pl.ds(at, 16)
            normed, inverse, active, slope = norm_gelu(r["z0"][rows])
            r["z0"][rows] = normed
            r["s0"][rows] = slope
            r["r0"][rows] = jnp.broadcast_to(inverse, (16, 128))
            narrow = active.astype(BF16)
            if c < 3:
                r["p1"][here, c * D : (c + 1) * D] = narrow
            if c == 0:
                r["shift"][here] = active
            else:
                odd = pl.ds(pl.multiple_of(ROWS + m * 16, 16), 16)
                if c >= 2:
                    r["p1"][odd, (c - 2) * D : (c - 1) * D] = narrow
            return carry

        lax.fori_loop(0, ROWS // 16, body, 0)
    r["shift"][ROWS : ROWS + 8] = jnp.zeros((8, D), F32)

    def shifted(m, carry):
        rows = pl.ds(pl.multiple_of(8 + m * 16, 8), 16)
        odd = pl.ds(pl.multiple_of(ROWS + m * 16, 16), 16)
        r["p1"][odd, 2 * D :] = r["shift"][rows].astype(BF16)
        return carry

    lax.fori_loop(0, ROWS // 16, shifted, 0)


def forward_second(w1_ref, r):
    r["z1"][...] = mm(r["p1"][...], w1_ref[...], NT)

    def even(m, carry):
        rows = pl.ds(pl.multiple_of(m * 16, 16), 16)
        normed, inverse, active, slope = norm_gelu(r["z1"][rows])
        r["z1"][rows] = normed
        r["s1"][rows] = slope
        r["r1"][rows] = jnp.broadcast_to(inverse, (16, 128))
        r["shift"][rows] = active
        return carry

    lax.fori_loop(0, ROWS // 16, even, 0)

    def odd(m, carry):
        rows = pl.ds(pl.multiple_of(ROWS + m * 16, 16), 16)
        here = pl.ds(pl.multiple_of(m * 16, 16), 16)
        normed, inverse, active, slope = norm_gelu(r["z1"][rows])
        r["z1"][rows] = normed
        r["s1"][rows] = slope
        r["r1"][rows] = jnp.broadcast_to(inverse, (16, 128))
        r["p2"][here, D : 2 * D] = active.astype(BF16)
        return carry

    lax.fori_loop(0, ROWS // 16, odd, 0)

    def spread(m, carry):
        here = pl.ds(pl.multiple_of(m * 16, 16), 16)
        after = pl.ds(pl.multiple_of(8 + m * 16, 8), 16)
        r["p2"][here, 0:D] = r["shift"][here].astype(BF16)
        r["p2"][here, 2 * D :] = r["shift"][after].astype(BF16)
        return carry

    lax.fori_loop(0, ROWS // 16, spread, 0)


def third_layer(cot_ref, w2_ref, r):
    r["z2"][...] = mm(r["p2"][0:ROWS2], w2_ref[...], NT)
    row, column = iota((ROWS2, ROWS2), 0), iota((ROWS2, ROWS2), 1)
    order = jnp.where(column == (row % SEG) * F2 + row // SEG, 1.0, 0.0).astype(BF16)
    r["c2"][...] = mm(order, cot_ref[...], NN)
    limit = jnp.concatenate([r["info"][0:8, 0:1]] * 2, axis=0)
    tokens = jnp.concatenate([r["info"][8:16, 0:1]] * 2, axis=0)
    half = (iota((16, 1), 0) // 8).astype(F32)

    def body(m, carry):
        rows = pl.ds(pl.multiple_of(m * 16, 16), 16)
        normed, inverse, active, slope = norm_gelu(r["z2"][rows])
        frame = half + (2 * m).astype(F32)
        weight = jnp.where(frame < limit, tokens, 0.0)
        grad = r["c2"][rows] * weight * slope
        r["d2"][rows] = norm_back(grad, normed, inverse).astype(BF16)
        return carry

    lax.fori_loop(0, ROWS2 // 16, body, 0)


def grad_third(out_ref, r):
    out_ref[...] = mm(r["d2"][...], r["p2"][0:ROWS2], TN).astype(out_ref.dtype)


def back_second(w2_ref, r):
    r["u"][0:8] = jnp.zeros((8, 3 * D), F32)
    r["u"][8 + ROWS2 : 32 + ROWS2] = jnp.zeros((24, 3 * D), F32)
    r["u"][8 : 8 + ROWS2] = mm(r["d2"][...], w2_ref[...], NN)

    def even(m, carry):
        rows = pl.ds(pl.multiple_of(m * 16, 16), 16)
        after = pl.ds(pl.multiple_of(8 + m * 16, 8), 16)
        up = r["u"][after, 0:D] + r["u"][rows, 2 * D :]
        delta = norm_back(up * r["s1"][rows], r["z1"][rows], r["r1"][rows, 0:1])
        r["d1"][rows] = delta.astype(BF16)
        return carry

    lax.fori_loop(0, ROWS // 16, even, 0)

    def odd(m, carry):
        rows = pl.ds(pl.multiple_of(ROWS + m * 16, 16), 16)
        after = pl.ds(pl.multiple_of(8 + m * 16, 8), 16)
        up = r["u"][after, D : 2 * D]
        delta = norm_back(up * r["s1"][rows], r["z1"][rows], r["r1"][rows, 0:1])
        r["d1"][rows] = delta.astype(BF16)
        return carry

    lax.fori_loop(0, ROWS // 16, odd, 0)


def grad_second(out_ref, r):
    out_ref[...] = mm(r["d1"][...], r["p1"][...], TN).astype(out_ref.dtype)


def back_first(w1_ref, r):
    r["ue"][...] = mm(r["d1"][0:ROWS], w1_ref[...], NN)
    r["uo"][0:8] = jnp.zeros((8, 3 * D), F32)
    r["uo"][8:] = mm(r["d1"][ROWS:], w1_ref[...], NN)
    for c in range(4):

        def body(m, carry, c=c):
            here = pl.ds(pl.multiple_of(m * 16, 16), 16)
            after = pl.ds(pl.multiple_of(8 + m * 16, 8), 16)
            rows = pl.ds(pl.multiple_of(c * ROWS + m * 16, 16), 16)
            if c == 0:
                up = r["ue"][here, 0:D] + r["uo"][here, 2 * D :]
            elif c == 1:
                up = r["ue"][here, D : 2 * D]
            elif c == 2:
                up = r["ue"][here, 2 * D :] + r["uo"][after, 0:D]
            else:
                up = r["uo"][after, D : 2 * D]
            delta = norm_back(up * r["s0"][rows], r["z0"][rows], r["r0"][rows, 0:1])
            r["d0"][rows] = delta.astype(BF16)
            return carry

        lax.fori_loop(0, ROWS // 16, body, 0)


def grad_first(out_ref, r):
    found = mm(r["d0"][...], r["x4"][...], TN)
    found = found + pltpu.roll(found, 96, axis=1)
    found = jnp.where(iota((D, 128), 1) < 10, found, 0.0)
    out_ref[...] = found.astype(out_ref.dtype)


COMPUTE_SCRATCH = {
    "x4": ((4 * ROWS, 128), BF16),
    "z0": ((4 * ROWS, D), F32),
    "s0": ((4 * ROWS, D), F32),
    "r0": ((4 * ROWS, 128), F32),
    "d0": ((4 * ROWS, D), BF16),
    "info": ((16, 128), F32),
    "shift": ((ROWS + 8, D), F32),
    "p1": ((2 * ROWS, 3 * D), BF16),
    "z1": ((2 * ROWS, D), F32),
    "s1": ((2 * ROWS, D), F32),
    "r1": ((2 * ROWS, 128), F32),
    "d1": ((2 * ROWS, D), BF16),
    "p2": ((ROWS, 3 * D), BF16),
    "z2": ((ROWS2, D), F32),
    "c2": ((ROWS2, D), F32),
    "d2": ((ROWS2, D), BF16),
    "u": ((ROWS2 + 32, 3 * D), F32),
    "ue": ((ROWS, 3 * D), F32),
    "uo": ((ROWS + 8, 3 * D), F32),
}


def compute_kernel(got, w0, w1, w2, cot, grads, *scratch):
    r = dict(zip(COMPUTE_SCRATCH, scratch))
    forward_first(got[...], w0, r)
    forward_second(w1, r)
    third_layer(cot, w2, r)
    grad_third(grads.at[:, 0 : 3 * D], r)
    back_second(w2, r)
    grad_second(grads.at[:, 3 * D : 6 * D], r)
    back_first(w1, r)
    grad_first(grads.at[:, 6 * D :], r)


def compute(got, w0, w1, w2, cot):
    vmem = pl.BlockSpec(memory_space=pltpu.VMEM)
    return pl.pallas_call(
        compute_kernel,
        out_shape=jax.ShapeDtypeStruct((D, 6 * D + 128), BF16),
        in_specs=[vmem] * 5,
        out_specs=vmem,
        scratch_shapes=[pltpu.VMEM(s, t) for s, t in COMPUTE_SCRATCH.values()],
        compiler_params=pltpu.CompilerParams(vmem_limit_bytes=56 << 20),
        cost_estimate=pl.CostEstimate(flops=3000000000, bytes_accessed=8000000, transcendentals=1400000),
    )(got, w0, w1, w2, cot)


def place():
    dp, batch = lax.axis_index("dp"), lax.axis_index("batch")
    return dp, batch, dp // 2, dp % 2, batch // 4, batch % 4


def signal_to(sem, dp, batch):
    pl.semaphore_signal(sem, inc=1, device_id=(dp, batch), device_id_type=pl.DeviceIdType.MESH)


def remote(src, dst, send, recv, dp, batch):
    return pltpu.make_async_remote_copy(
        src_ref=src,
        dst_ref=dst,
        send_sem=send,
        recv_sem=recv,
        device_id=(dp, batch),
        device_id_type=pl.DeviceIdType.MESH,
    )


def landed(ref, sem):
    pltpu.make_async_copy(ref, ref, sem).wait()


def loop(first, last, step):
    def body(i, carry):
        step(i)
        return carry

    lax.fori_loop(first, last, body, 0)


def pack_waves(wave, dest, length, tokens):
    high = wave.astype(BF16).astype(F32)
    low = wave - high
    lane, row = iota((SEG, 128), 1), iota((SEG, 128), 0)
    target = lane // 32 * 8 + (lane // 8) % 4
    extra = jnp.zeros((SEG, 128), F32)
    for s in range(SEG):
        here = dest[s]
        rank = 0
        for t in range(s):
            rank = rank + jnp.where(dest[t] == here, 1, 0)
        target = target + jnp.where(lane % 8 == s, here * 16 + rank * 4, 0)
        detail = jnp.where(lane == 126, length[s] - 256, tokens[s]).astype(F32)
        extra = jnp.where(row == s, detail, extra)
    rows = [high[:, 128 * i : 128 * i + 128] for i in range(4)]
    rows += [low[:, 128 * i : 128 * i + 128] for i in range(3)]
    rows.append(jnp.where(lane < 126, low[:, 384:], extra))
    data = jnp.concatenate(rows, axis=0).astype(BF16)
    select = jnp.where(iota((512, 64), 0) == target[0:1, 0:64], 1.0, 0.0).astype(BF16)
    return mm(select, data, NN).astype(BF16)


def exchange_kernel(
    wave, dest, length, tokens, w0, w1, w2, got, f0, f1, f2,
    send, mine0, wave_send, wave_recv, row_send, row_recv, pass_send, pass_recv,
):
    dp, batch, y, core, z, x = place()
    barrier = pltpu.get_barrier_semaphore()
    loop(1, 32, lambda k: signal_to(barrier, dp, lax.rem(batch + k, 32)))
    for k in range(1, 4):
        signal_to(barrier, lax.rem(y + k, 4) * 2 + core, batch)
    signal_to(barrier, y * 2 + 1 - core, batch)
    mine0[...] = jnp.concatenate([w0[...], jnp.zeros((64, 118), BF16)], axis=1)
    send[...] = pack_waves(wave[...], dest, length, tokens).reshape(32, 16, 128)
    pl.semaphore_wait(barrier, 35)

    def wave_copy(k):
        to = lax.rem(batch + k, 32)
        return remote(send.at[to], got.at[batch], wave_send, wave_recv, dp, to)

    loop(1, 32, lambda k: wave_copy(k).start())
    sources, fulls = (mine0, w1, w2), (f0, f1, f2)

    def block(full, who):
        return full.at[pl.ds(pl.multiple_of(who * 64, 64), 64)]

    def row_copy(w, k):
        to = lax.rem(y + k, 4) * 2 + core
        return remote(sources[w], block(fulls[w], dp), row_send.at[w, k], row_recv.at[w, k], to, batch)

    def pass_copy(w, k):
        owner = lax.rem(y + 4 - k, 4) * 2 + core
        source = sources[w] if k == 0 else block(fulls[w], owner)
        to = y * 2 + 1 - core
        return remote(source, block(fulls[w], owner), pass_send.at[w, k], pass_recv.at[w, k], to, batch)

    for w in range(3):
        for k in (2, 1, 3):
            row_copy(w, k).start()
        pass_copy(w, 0).start()
    got[batch] = send[batch]
    for w in range(3):
        block(fulls[w], dp)[...] = sources[w][...]
    for w in range(3):
        for k in (1, 3, 2):
            row_copy(w, k).wait_recv()
            pass_copy(w, k).start()
    landed(send.at[0:31], wave_recv)
    landed(send.at[0:31], wave_send)
    for w in range(3):
        for k in range(4):
            pass_copy(w, k).wait()
            if k:
                row_copy(w, k).wait_send()


def exchange(wave, dest, length, tokens, w0, w1, w2):
    vmem = pl.BlockSpec(memory_space=pltpu.VMEM)
    smem = pl.BlockSpec(memory_space=pltpu.SMEM)
    return pl.pallas_call(
        exchange_kernel,
        out_shape=(
            jax.ShapeDtypeStruct((32, 16, 128), BF16),
            jax.ShapeDtypeStruct((D, 128), BF16),
            jax.ShapeDtypeStruct((D, 3 * D), BF16),
            jax.ShapeDtypeStruct((D, 3 * D), BF16),
        ),
        in_specs=[vmem, smem, smem, smem, vmem, vmem, vmem],
        out_specs=(vmem,) * 4,
        scratch_shapes=[
            pltpu.VMEM((32, 16, 128), BF16),
            pltpu.VMEM((64, 128), BF16),
            pltpu.SemaphoreType.DMA,
            pltpu.SemaphoreType.DMA,
            pltpu.SemaphoreType.DMA((3, 4)),
            pltpu.SemaphoreType.DMA((3, 4)),
            pltpu.SemaphoreType.DMA((3, 4)),
            pltpu.SemaphoreType.DMA((3, 4)),
        ],
        compiler_params=pltpu.CompilerParams(
            collective_id=0, has_side_effects=True, vmem_limit_bytes=40 << 20
        ),
    )(wave, dest, length, tokens, w0, w1, w2)


WIDE = 6 * D + 128
PIECES = ((0, 3 * D), (3 * D, 3 * D), (6 * D, 128))
COUNT = D * 10 + 6 * D * D


def reduce_kernel(
    grads, tokens, out,
    rc, ys, yr, xs, xr, zs, zr, fz, fx, fr, ta, tb, sa, sb, my_t, my_t2, my_s, my_s2,
    core_send, core_recv, y_send, y_recv, x_send, x_recv, z_send, z_recv, fz_send, fz_recv, fx_send, fx_recv,
    ta_send, ta_recv, tb_send, tb_recv, sa_send, sa_recv, sb_send, sb_recv,
):
    dp, batch, y, core, z, x = place()
    barrier = pltpu.get_barrier_semaphore()
    group = dp * 4 + x

    def group_peer(k):
        other = lax.rem(group + k, 32)
        return other // 4, z * 4 + other % 4

    def z_peer(k):
        return lax.rem(z + k, 8) * 4 + x

    def x_peer(k):
        return z * 4 + lax.rem(x + k, 4)

    loop(1, 32, lambda k: signal_to(barrier, *group_peer(k)))
    loop(1, 8, lambda k: signal_to(barrier, dp, z_peer(k)))
    total = tokens[0]
    for s in range(1, SEG):
        total = total + tokens[s]
    my_t[...] = jnp.broadcast_to(total.astype(F32), (8, 128))
    pl.semaphore_wait(barrier, 38)

    def core_copy(p, k):
        start, width = PIECES[p]
        step = lax.rem(y + k, 4)
        rows = pl.ds(pl.multiple_of((step * 2 + 1 - core) * 64, 64), 64)
        return remote(
            grads.at[rows, start : start + width], rc.at[step, :, start : start + width],
            core_send.at[p, k], core_recv.at[p, k], y * 2 + 1 - core, batch,
        )

    def y_copy(p, k):
        start, width = PIECES[p]
        to = lax.rem(y + k, 4)
        return remote(
            ys.at[to, :, start : start + width], yr.at[y, :, start : start + width],
            y_send.at[p, k], y_recv.at[p, k], to * 2 + core, batch,
        )

    def x_copy(k):
        to = lax.rem(x + k, 4)
        return remote(
            xs.at[pl.ds(pl.multiple_of(to * 16, 16), 16)], xr.at[x],
            x_send.at[k], x_recv.at[k], dp, z * 4 + to,
        )

    def z_copy(k):
        to = lax.rem(z + k, 8)
        return remote(zs.at[to], zr.at[z], z_send, z_recv, dp, to * 4 + x)

    def fz_copy(k):
        return remote(fz.at[z], fz.at[z], fz_send, fz_recv, dp, z_peer(k))

    def fx_copy(k):
        return remote(fr.at[x], fr.at[x], fx_send, fx_recv, dp, x_peer(k))

    def ta_copy(k):
        return remote(my_t, ta.at[group], ta_send, ta_recv, *group_peer(k))

    def tb_copy(k):
        return remote(my_t2, tb.at[z], tb_send, tb_recv, dp, z_peer(k))

    def sa_copy(k):
        return remote(my_s, sa.at[z], sa_send, sa_recv, dp, z_peer(k))

    def sb_copy(k):
        return remote(my_s2, sb.at[group], sb_send, sb_recv, *group_peer(k))

    for p in range(3):
        for k in (2, 1, 3, 0):
            core_copy(p, k).start()
    loop(1, 32, lambda k: ta_copy(k).start())
    ta[group] = my_t[...]
    for p in range(3):
        start, width = PIECES[p]
        for k in (2, 1, 3, 0):
            core_copy(p, k).wait_recv()
            step = lax.rem(y + k, 4)
            rows = pl.ds(pl.multiple_of((step * 2 + core) * 64, 64), 64)
            own = grads[rows, start : start + width].astype(F32)
            ys[step, :, start : start + width] = (
                own + rc[step, :, start : start + width].astype(F32)
            ).astype(BF16)
            if k:
                y_copy(p, k).start()
    landed(ta.at[0:31], ta_recv)
    my_t2[...] = jnp.sum(ta[...], axis=0)
    tb[z] = my_t2[...]
    loop(1, 8, lambda k: tb_copy(k).start())
    for p in range(3):
        start, width = PIECES[p]
        found = ys[y, :, start : start + width].astype(F32)
        for k in (1, 3, 2):
            y_copy(p, k).wait_recv()
            found = found + yr[lax.rem(y + 4 - k, 4), :, start : start + width].astype(F32)
        xs[:, start : start + width] = found.astype(BF16)
    for k in (2, 1, 3):
        x_copy(k).start()
    found = xs[pl.ds(pl.multiple_of(x * 16, 16), 16)].astype(F32)
    for k in (1, 3, 2):
        x_copy(k).wait_recv()
        found = found + xr[lax.rem(x + 4 - k, 4)].astype(F32)
    for q in range(8):
        zs[q, :, 0:384] = found[:, q * 384 : q * 384 + 384].astype(BF16)
        zs[q, :, 384:] = found[:, 6 * D :].astype(BF16)
    loop(1, 8, lambda k: z_copy(k).start())
    zr[z] = zs[z]
    landed(tb.at[0:7], tb_recv)
    token_sum = jnp.sum(tb[...], axis=0)
    landed(zr.at[0:7], z_recv)
    found = jnp.sum(zr[...].astype(F32), axis=0)
    fz[z] = found[:, 0:384].astype(BF16)
    loop(1, 8, lambda k: fz_copy(k).start())
    scaled = found * (1.0 / token_sum[0:1, 0:1])
    own = jnp.sum(scaled[:, 0:384] * scaled[:, 0:384], keepdims=True)
    first = jnp.sum(scaled[:, 384:] * scaled[:, 384:], keepdims=True)
    my_s[...] = jnp.broadcast_to(own + jnp.where(z == 0, first, 0.0), (8, 128))
    loop(1, 8, lambda k: sa_copy(k).start())
    sa[z] = my_s[...]
    fr[x, :, 6 * D :] = found[:, 384:].astype(BF16)
    landed(fz.at[0:7], fz_recv)
    for q in range(8):
        fr[x, :, q * 384 : q * 384 + 384] = fz[q]
    for k in (2, 1, 3):
        fx_copy(k).start()
    landed(sa.at[0:7], sa_recv)
    my_s2[...] = jnp.sum(sa[...], axis=0)
    loop(1, 32, lambda k: sb_copy(k).start())
    sb[group] = my_s2[...]
    landed(sb.at[0:31], sb_recv)
    squares = jnp.sum(sb[...], axis=0)
    rms = jnp.sqrt(squares * (1.0 / COUNT))
    factor = (1.0 / (token_sum * jnp.maximum(rms, 1.0)))[0:1, 0:1]
    landed(fr.at[0:3], fx_recv)
    out[0:64] = fr[...].reshape(64, WIDE).astype(F32) * factor
    out[64:72] = jnp.broadcast_to(rms[0:1, 0:1], (8, WIDE))
    for p in range(3):
        for k in range(4):
            core_copy(p, k).wait_send()
            if k:
                y_copy(p, k).wait_send()
    for k in range(1, 4):
        x_copy(k).wait_send()
    landed(zr.at[0:7], z_send)
    landed(fz.at[0:7], fz_send)
    landed(fr.at[0:3], fx_send)
    landed(ta.at[0:31], ta_send)
    landed(sb.at[0:31], sb_send)
    landed(tb.at[0:7], tb_send)
    landed(sa.at[0:7], sa_send)


def reduce_grads(grads, tokens):
    vmem = pl.BlockSpec(memory_space=pltpu.VMEM)
    smem = pl.BlockSpec(memory_space=pltpu.SMEM)
    dma = pltpu.SemaphoreType.DMA
    return pl.pallas_call(
        reduce_kernel,
        out_shape=jax.ShapeDtypeStruct((72, WIDE), F32),
        in_specs=[vmem, smem],
        out_specs=vmem,
        scratch_shapes=[
            pltpu.VMEM((4, 64, WIDE), BF16),
            pltpu.VMEM((4, 64, WIDE), BF16),
            pltpu.VMEM((4, 64, WIDE), BF16),
            pltpu.VMEM((64, WIDE), BF16),
            pltpu.VMEM((4, 16, WIDE), BF16),
            pltpu.VMEM((8, 16, 512), BF16),
            pltpu.VMEM((8, 16, 512), BF16),
            pltpu.VMEM((8, 16, 384), BF16),
            pltpu.VMEM((16, WIDE), BF16),
            pltpu.VMEM((4, 16, WIDE), BF16),
            pltpu.VMEM((32, 8, 128), F32),
            pltpu.VMEM((8, 8, 128), F32),
            pltpu.VMEM((8, 8, 128), F32),
            pltpu.VMEM((32, 8, 128), F32),
        ]
        + [pltpu.VMEM((8, 128), F32)] * 4
        + [dma((3, 4))] * 4
        + [dma((4,))] * 2
        + [dma] * 14,
        compiler_params=pltpu.CompilerParams(
            collective_id=1, has_side_effects=True, vmem_limit_bytes=40 << 20
        ),
    )(grads, tokens)


def local(wave, length, dest, tokens, cot, w0, w1, w2):
    got, f0, f1, f2 = exchange(wave, dest, length, tokens, w0, w1, w2)
    grads = compute(got.reshape(512, 128), f0, f1, f2, cot.reshape(ROWS2, D))
    out = reduce_grads(grads, tokens)
    return (
        out[0:64, 6 * D : 6 * D + 10],
        out[0:64, 3 * D : 6 * D],
        out[0:64, 0 : 3 * D],
        out[64, 0:1],
    )


def solution(mesh):
    row = P(("dp", "batch"))
    return jax.shard_map(
        local,
        mesh=mesh,
        in_specs=(row, row, row, row, row, P("dp"), P("dp"), P("dp")),
        out_specs=(P("dp"), P("dp"), P("dp"), P()),
        check_vma=False,
    )
```

time: 447 us -> 137 us (0.31)
  waiting for transfers between devices: 186 us -> 0 us
  blocking collectives: 155 us -> 0 us
  Pallas kernels: 0 us -> 123 us
  other arithmetic: 25.2 us -> 0 us
  starting transfers between devices: 21.8 us -> 0 us
  matrix products: 19.9 us -> 0 us
  between operations: 19.2 us -> 0.67 us
  local copies, waits for them, and re-layouts: 19.1 us -> 13.1 us
    psum x2 -> x0, blocking collectives: 141 us -> none  [the longest x1 79 us: local(): square_sum = lax.psum(square_part, ('dp', 'batch'))]
    pallas_call x0 -> x3, Pallas kernels: none -> 123 us  [the longest x1 50.9 us: reduce_grads(): pl.pallas_call(reduce_kernel, out_shape=jax.ShapeDtypeStruct((72, WIDE),...]
    psum x1 -> x0, waiting for transfers between devices: 85.4 us -> none  [local(): owned = lax.psum((owner_part[0], owner_part[1], owner_part[2]), 'batch')]
    reduce_scatter x2 -> x0, waiting for transfers between devices: 55.7 us -> none  [the longest x1 39.5 us: local(): lax.psum_scatter(sums[2], 'dp', scatter_dimension=0, tiled=True)]
    unnamed x7 -> x0, waiting for transfers between devices: 36 us -> none
    all_to_all x2 -> x0, starting transfers between devices: 21.4 us -> none  [the longest x1 11.9 us: local(): lax.all_to_all(send_detail, 'batch', split_axis=0, concat_axis=0, tiled=T...]
    dot_general x11 -> x0, matrix products: 19 us -> none  [the longest x1 4.6 us: segment_gradient_list(): jnp.einsum('sfc,sfk->ck', delta_zero, patches0, precision=lax.Precision.H...]
    all_gather x1 -> x0, blocking collectives: 14.2 us -> none  [local(): lax.all_gather(initial_filter_weight, 'dp', axis=0, tiled=True)]
  transfers between devices with their start and end apart: 8 -> 0, of which waited for: 5 -> 0; matrix products, arithmetic and copies ran while one was open for 9% -> 0% of each run, Pallas kernels for 0% -> 0%
where the time goes in v1:
time: 137 us
  Pallas kernels  123 us (90%)
  local copies, waits for them, and re-layouts  13.1 us (10%)
    pallas_call x1, Pallas kernels, reduce_grads(): pl.pallas_call(reduce_kernel, out_shape=jax.ShapeDtypeStruct((72, WIDE),...  50.9 us
    pallas_call x1, Pallas kernels, compute(): pl.pallas_call(compute_kernel, out_shape=jax.ShapeDtypeStruct((D, 6 * D +...  36.9 us
    pallas_call x1, Pallas kernels, exchange(): pl.pallas_call(exchange_kernel, out_shape=(jax.ShapeDtypeStruct((32, 16,...  35.1 us
    unnamed x26, local copies, waits for them, and re-layouts  11.6 us

profile of v1, /device:TPU:1, one launch (start us, length us, event | category | flops | bytes accessed | tf_op | source)
XLA Modules:
  0.0 136.6 jit_solution(11499270432397602341)
XLA Ops:
  0.6 0.8 copy.12.w0
  1.4 0.0 copy-start.1
  1.4 0.9 copy-done.1
  2.4 0.0 copy-start.2
  2.4 0.9 copy-done.2
  3.3 0.0 copy-start.3
  3.3 0.7 copy-done.3
  4.0 0.0 copy-start.4
  4.0 0.7 copy-done.4
  4.7 0.7 copy-done.6
  5.3 0.7 copy-done.7
  6.0 35.1 %shard_map.111 = (bf16[32,16,128]{2,1,0:T(8,128)(2,1)S(1)}, bf16[512,128]{1,0:T(8,128)(2,1)S(1)}, bf16[512,1536]{1,0:T(8,128)(2,1)S(1)}, bf16[512,1536]{1,0:T(8,128)(2,1)S(1)}) custom-call(f32[8,512]{1,0:T(8,128)S(1)} %copy-done.3, s32[8]{0:T(128)S(1)} %copy-done.6, s32[8]{0:T(128)S(1)} %copy-done.7, s32[8]{0:T(128)S(1)} %copy-done.4, ...), custom_call_target="tpu_custom_call" | custom-call | tf_op jit(solution)/shard_map/pallas_call | solution.py:431
  41.0 0.0 copy-start.8
  41.0 1.1 copy-done.8
  42.2 1.2 copy-done.9
  43.4 0.7 copy-done.10
  44.0 0.7 copy-done.11
  44.7 36.9 %shard_map.112.grads = bf16[512,3200]{1,0:T(8,128)(2,1)} custom-call(bf16[512,128]{1,0:T(8,128)(2,1)} %bitcast.3, bf16[512,128]{1,0:T(8,128)(2,1)} %copy-done.11, bf16[512,1536]{1,0:T(8,128)(2,1)} %copy-done.8, bf16[512,1536]{1,0:T(8,128)(2,1)} %copy-done.9, bf16[192,512]{1,0:T(8,128)(2,1)} %bitcast.4), custom_call_target="tpu_custom_call" | custom-call | flops 3000000000 | bytes 8000000 | tf_op jit(solution)/shard_map/pallas_call | solution.py:309
  81.6 0.0 copy-done.5
  81.6 1.9 %copy-done = bf16[512,3200]{1,0:T(8,128)(2,1)S(1)} copy-done((bf16[512,3200]{1,0:T(8,128)(2,1)S(1)}, bf16[512,3200]{1,0:T(8,128)(2,1)}, u32[]{:S(2)}) %copy-start) | copy-done | bytes 3276824
  83.5 50.9 %shard_map.113 = f32[72,3200]{1,0:T(8,128)S(1)} custom-call(bf16[512,3200]{1,0:T(8,128)(2,1)S(1)} %copy-done, s32[8]{0:T(128)S(1)} %copy-done.5), custom_call_target="tpu_custom_call" | custom-call | tf_op jit(solution)/shard_map/pallas_call | solution.py:624
  134.4 0.5 slice.15
  134.9 1.0 fusion
  135.9 0.7 copy.13
  (8 shorter events, 0.0 us)
Async XLA Ops:
  1.4 0.9 copy-start.1
  2.4 0.9 copy-start.2
  3.3 0.7 copy-start.3
  4.0 0.7 copy-start.4
  4.7 0.7 copy-start.6
  5.3 0.7 copy-start.7
  41.0 1.2 copy-start.8
  42.2 1.2 copy-start.9
  43.4 0.7 copy-start.10
  44.0 0.7 copy-start.11
  44.7 36.9 %copy-start.5 = (s32[8]{0:T(128)S(1)}, s32[8]{0:T(128)}, u32[]{:S(2)}) copy-start(s32[8]{0:T(128)} %tokens.3) | copy-start | bytes 100
  81.6 1.9 %copy-start = (bf16[512,3200]{1,0:T(8,128)(2,1)S(1)}, bf16[512,3200]{1,0:T(8,128)(2,1)}, u32[]{:S(2)}) copy-start(bf16[512,3200]{1,0:T(8,128)(2,1)} %shard_map.112.grads) | copy-start | bytes 9830404

commit v2 on v1

v2 whole, which is shorter than its diff:
```python
import functools

import jax
import jax.numpy as jnp
from jax import lax
from jax.experimental import pallas as pl
from jax.experimental.pallas import tpu as pltpu
from jax.sharding import PartitionSpec as P

F32 = jnp.float32
BF16 = jnp.bfloat16
D = 512
SEG = 8
J = 26
ROWS = J * SEG
F2 = 24
UNROLL = True
ROWS2 = F2 * SEG
NT = (((1,), (1,)), ((), ()))
TN = (((0,), (0,)), ((), ()))
NN = (((1,), (0,)), ((), ()))


def mm(a, b, dims):
    return lax.dot_general(a, b, dims, preferred_element_type=F32)


def iota(shape, dim):
    return lax.broadcasted_iota(jnp.int32, shape, dim)


def mean(x):
    return jnp.sum(x, axis=-1, keepdims=True) * (1.0 / D)


def norm_gelu(hidden):
    centred = hidden - mean(hidden)
    inverse = lax.rsqrt(mean(centred * centred) + 1e-05)
    normed = centred * inverse
    cdf = 0.5 + 0.5 * lax.erf(normed * 0.7071067811865476)
    slope = cdf + normed * jnp.exp(-0.5 * normed * normed) * 0.3989422804014327
    return normed, inverse, normed * cdf, slope


def norm_back(grad, normed, inverse):
    return inverse * (grad - mean(grad) - normed * mean(grad * normed))


def pick_waves(got):
    lane_pick = (iota((SEG, 128), 1) == 127).astype(BF16)
    token_row = mm(lane_pick, got, NT)
    column = iota((SEG, 512), 1)
    carries = jnp.logical_and(column % 16 >= 8, column % 4 == 3)
    filled = jnp.where(jnp.logical_and(carries, token_row > 0.5), 1.0, 0.0).astype(BF16)
    row_slot = iota((512, 512), 0)
    row_slot = (row_slot // 16) * 2 + (row_slot // 4) % 2
    column_slot = iota((512, 512), 1)
    column_slot = (column_slot // 16) * 2 + (column_slot // 4) % 2
    weight = jnp.where(row_slot < column_slot, 1.0, 0.0) + jnp.where(
        row_slot == column_slot, 64.0, 0.0
    )
    place = mm(filled, weight.astype(BF16), NN) - 64.0
    target = place + ((column // 8) % 2 * 32 + (column % 4) * 8).astype(F32)
    target = jnp.where(place > -0.5, target, -1.0)
    picking = jnp.where(iota((64, 512), 0).astype(F32) == target[0:1], 1.0, 0.0).astype(BF16)
    picked = mm(picking, got, NN)
    last = picked[56:64]
    length = last[:, 126:127] + 256.0
    tokens = last[:, 127:128]
    low_last = jnp.where(iota((SEG, 128), 1) < 126, last, 0.0)
    pieces = [picked[8 * i : 8 * i + 8] + picked[32 + 8 * i : 40 + 8 * i] for i in range(3)]
    pieces.append(picked[24:32] + low_last)
    return jnp.concatenate(pieces, axis=1), length, tokens


def first_taps(wave, length):
    inside = iota((SEG, D), 1).astype(F32) < length
    average = jnp.sum(jnp.where(inside, wave, 0.0), axis=1, keepdims=True) / length
    centred = jnp.where(inside, wave - average, 0.0)
    variance = jnp.sum(centred * centred, axis=1, keepdims=True) / length
    normal = centred * lax.rsqrt(variance + 1e-07)
    padded = jnp.concatenate([normal, jnp.zeros((SEG, 256), F32)], axis=1)
    rows = []
    for j in range(J):
        tile, shift = (20 * j) // 128, (20 * j) % 128
        pair = padded[:, tile * 128 : tile * 128 + 256]
        if shift:
            pair = pltpu.roll(pair, 256 - shift, axis=1)
        rows.append(pair[:, :128])
    taps = jnp.concatenate(rows, axis=0)
    return jnp.where(iota((ROWS, 128), 1) < 32, taps, 0.0)


def forward_first(got, w0_ref, r):
    wave, length, tokens = pick_waves(got)
    taps = first_taps(wave, length)
    high = taps.astype(BF16).astype(F32)
    both = high + pltpu.roll(taps - high, 32, axis=1)
    both_narrow = both.astype(BF16)
    narrow_lane = iota((ROWS, 128), 1)
    for c in range(4):
        moved = pltpu.roll(both, 128 - 5 * c, axis=1) if c else both
        keep = narrow_lane % 32 < 10
        moved = jnp.where(jnp.logical_and(keep, narrow_lane < 64), moved, 0.0)
        r["x4"][c * ROWS : (c + 1) * ROWS] = moved.astype(BF16)
    w0 = w0_ref[...]
    tap_row, tap_column = iota((128, 128), 0), iota((128, 128), 1)
    for c in range(4):
        placing = jnp.logical_and(tap_row % 32 == tap_column + 5 * c, tap_row < 64)
        placing = jnp.logical_and(placing, tap_column < 10)
        weight = mm(jnp.where(placing, 1.0, 0.0).astype(BF16), w0, NT).astype(BF16)
        r["z0"][c * ROWS : (c + 1) * ROWS] = mm(both_narrow, weight, NN)
    l2 = ((((length - 10.0) * 0.2).astype(jnp.int32) + 1 - 3) // 2 + 1 - 3) // 2 + 1
    r["info"][0:8] = jnp.broadcast_to(l2.astype(F32), (SEG, 128))
    r["info"][8:16] = jnp.broadcast_to(tokens, (SEG, 128))

    for c in range(4):

        def body(m, carry, c=c):
            at = pl.multiple_of(m * 16, 16)
            rows = pl.ds(pl.multiple_of(c * ROWS + m * 16, 16), 16)
            here = pl.ds(at, 16)
            normed, inverse, active, slope = norm_gelu(r["z0"][rows])
            r["z0"][rows] = normed
            r["s0"][rows] = slope
            r["r0"][rows] = jnp.broadcast_to(inverse, (16, 128))
            narrow = active.astype(BF16)
            if c < 3:
                r["p1"][here, c * D : (c + 1) * D] = narrow
            if c == 0:
                r["shift"][here] = active
            else:
                odd = pl.ds(pl.multiple_of(ROWS + m * 16, 16), 16)
                if c >= 2:
                    r["p1"][odd, (c - 2) * D : (c - 1) * D] = narrow
            return carry

        lax.fori_loop(0, ROWS // 16, body, 0, unroll=UNROLL)
    r["shift"][ROWS : ROWS + 8] = jnp.zeros((8, D), F32)

    def shifted(m, carry):
        rows = pl.ds(pl.multiple_of(8 + m * 16, 8), 16)
        odd = pl.ds(pl.multiple_of(ROWS + m * 16, 16), 16)
        r["p1"][odd, 2 * D :] = r["shift"][rows].astype(BF16)
        return carry

    lax.fori_loop(0, ROWS // 16, shifted, 0, unroll=UNROLL)


def forward_second(w1_ref, r):
    r["z1"][...] = mm(r["p1"][...], w1_ref[...], NT)

    def even(m, carry):
        rows = pl.ds(pl.multiple_of(m * 16, 16), 16)
        normed, inverse, active, slope = norm_gelu(r["z1"][rows])
        r["z1"][rows] = normed
        r["s1"][rows] = slope
        r["r1"][rows] = jnp.broadcast_to(inverse, (16, 128))
        r["shift"][rows] = active
        return carry

    lax.fori_loop(0, ROWS // 16, even, 0, unroll=UNROLL)

    def odd(m, carry):
        rows = pl.ds(pl.multiple_of(ROWS + m * 16, 16), 16)
        here = pl.ds(pl.multiple_of(m * 16, 16), 16)
        normed, inverse, active, slope = norm_gelu(r["z1"][rows])
        r["z1"][rows] = normed
        r["s1"][rows] = slope
        r["r1"][rows] = jnp.broadcast_to(inverse, (16, 128))
        r["p2"][here, D : 2 * D] = active.astype(BF16)
        return carry

    lax.fori_loop(0, ROWS // 16, odd, 0, unroll=UNROLL)

    def spread(m, carry):
        here = pl.ds(pl.multiple_of(m * 16, 16), 16)
        after = pl.ds(pl.multiple_of(8 + m * 16, 8), 16)
        r["p2"][here, 0:D] = r["shift"][here].astype(BF16)
        r["p2"][here, 2 * D :] = r["shift"][after].astype(BF16)
        return carry

    lax.fori_loop(0, ROWS // 16, spread, 0, unroll=UNROLL)


def third_layer(cot_ref, w2_ref, r):
    r["z2"][...] = mm(r["p2"][0:ROWS2], w2_ref[...], NT)
    row, column = iota((ROWS2, ROWS2), 0), iota((ROWS2, ROWS2), 1)
    order = jnp.where(column == (row % SEG) * F2 + row // SEG, 1.0, 0.0).astype(BF16)
    r["c2"][...] = mm(order, cot_ref[...], NN)
    limit = jnp.concatenate([r["info"][0:8, 0:1]] * 2, axis=0)
    tokens = jnp.concatenate([r["info"][8:16, 0:1]] * 2, axis=0)
    half = (iota((16, 1), 0) // 8).astype(F32)

    def body(m, carry):
        rows = pl.ds(pl.multiple_of(m * 16, 16), 16)
        normed, inverse, active, slope = norm_gelu(r["z2"][rows])
        frame = half + (2 * m).astype(F32)
        weight = jnp.where(frame < limit, tokens, 0.0)
        grad = r["c2"][rows] * weight * slope
        r["d2"][rows] = norm_back(grad, normed, inverse).astype(BF16)
        return carry

    lax.fori_loop(0, ROWS2 // 16, body, 0, unroll=UNROLL)


def grad_third(out_ref, r):
    out_ref[...] = mm(r["d2"][...], r["p2"][0:ROWS2], TN).astype(out_ref.dtype)


def back_second(w2_ref, r):
    r["u"][0:8] = jnp.zeros((8, 3 * D), F32)
    r["u"][8 + ROWS2 : 32 + ROWS2] = jnp.zeros((24, 3 * D), F32)
    r["u"][8 : 8 + ROWS2] = mm(r["d2"][...], w2_ref[...], NN)

    def even(m, carry):
        rows = pl.ds(pl.multiple_of(m * 16, 16), 16)
        after = pl.ds(pl.multiple_of(8 + m * 16, 8), 16)
        up = r["u"][after, 0:D] + r["u"][rows, 2 * D :]
        delta = norm_back(up * r["s1"][rows], r["z1"][rows], r["r1"][rows, 0:1])
        r["d1"][rows] = delta.astype(BF16)
        return carry

    lax.fori_loop(0, ROWS // 16, even, 0, unroll=UNROLL)

    def odd(m, carry):
        rows = pl.ds(pl.multiple_of(ROWS + m * 16, 16), 16)
        after = pl.ds(pl.multiple_of(8 + m * 16, 8), 16)
        up = r["u"][after, D : 2 * D]
        delta = norm_back(up * r["s1"][rows], r["z1"][rows], r["r1"][rows, 0:1])
        r["d1"][rows] = delta.astype(BF16)
        return carry

    lax.fori_loop(0, ROWS // 16, odd, 0, unroll=UNROLL)


def grad_second(out_ref, r):
    out_ref[...] = mm(r["d1"][...], r["p1"][...], TN).astype(out_ref.dtype)


def back_first(w1_ref, r):
    r["ue"][...] = mm(r["d1"][0:ROWS], w1_ref[...], NN)
    r["uo"][0:8] = jnp.zeros((8, 3 * D), F32)
    r["uo"][8:] = mm(r["d1"][ROWS:], w1_ref[...], NN)
    for c in range(4):

        def body(m, carry, c=c):
            here = pl.ds(pl.multiple_of(m * 16, 16), 16)
            after = pl.ds(pl.multiple_of(8 + m * 16, 8), 16)
            rows = pl.ds(pl.multiple_of(c * ROWS + m * 16, 16), 16)
            if c == 0:
                up = r["ue"][here, 0:D] + r["uo"][here, 2 * D :]
            elif c == 1:
                up = r["ue"][here, D : 2 * D]
            elif c == 2:
                up = r["ue"][here, 2 * D :] + r["uo"][after, 0:D]
            else:
                up = r["uo"][after, D : 2 * D]
            delta = norm_back(up * r["s0"][rows], r["z0"][rows], r["r0"][rows, 0:1])
            r["d0"][rows] = delta.astype(BF16)
            return carry

        lax.fori_loop(0, ROWS // 16, body, 0, unroll=UNROLL)


def grad_first(out_ref, r):
    found = mm(r["d0"][...], r["x4"][...], TN)
    found = found + pltpu.roll(found, 96, axis=1)
    found = jnp.where(iota((D, 128), 1) < 10, found, 0.0)
    out_ref[...] = found.astype(out_ref.dtype)


COMPUTE_SCRATCH = {
    "x4": ((4 * ROWS, 128), BF16),
    "z0": ((4 * ROWS, D), F32),
    "s0": ((4 * ROWS, D), F32),
    "r0": ((4 * ROWS, 128), F32),
    "d0": ((4 * ROWS, D), BF16),
    "info": ((16, 128), F32),
    "shift": ((ROWS + 8, D), F32),
    "p1": ((2 * ROWS, 3 * D), BF16),
    "z1": ((2 * ROWS, D), F32),
    "s1": ((2 * ROWS, D), F32),
    "r1": ((2 * ROWS, 128), F32),
    "d1": ((2 * ROWS, D), BF16),
    "p2": ((ROWS, 3 * D), BF16),
    "z2": ((ROWS2, D), F32),
    "c2": ((ROWS2, D), F32),
    "d2": ((ROWS2, D), BF16),
    "u": ((ROWS2 + 32, 3 * D), F32),
    "ue": ((ROWS, 3 * D), F32),
    "uo": ((ROWS + 8, 3 * D), F32),
}


def place():
    dp, batch = lax.axis_index("dp"), lax.axis_index("batch")
    return dp, batch, dp // 2, dp % 2, batch // 4, batch % 4


def signal_to(sem, dp, batch):
    pl.semaphore_signal(sem, inc=1, device_id=(dp, batch), device_id_type=pl.DeviceIdType.MESH)


def remote(src, dst, send, recv, dp, batch):
    return pltpu.make_async_remote_copy(
        src_ref=src,
        dst_ref=dst,
        send_sem=send,
        recv_sem=recv,
        device_id=(dp, batch),
        device_id_type=pl.DeviceIdType.MESH,
    )


def landed(ref, sem):
    pltpu.make_async_copy(ref, ref, sem).wait()


def loop(first, last, step):
    def body(i, carry):
        step(i)
        return carry

    lax.fori_loop(first, last, body, 0)


def pack_waves(wave, dest, length, tokens):
    high = wave.astype(BF16).astype(F32)
    low = wave - high
    lane, row = iota((SEG, 128), 1), iota((SEG, 128), 0)
    target = lane // 32 * 8 + (lane // 8) % 4
    extra = jnp.zeros((SEG, 128), F32)
    for s in range(SEG):
        here = dest[s]
        rank = 0
        for t in range(s):
            rank = rank + jnp.where(dest[t] == here, 1, 0)
        target = target + jnp.where(lane % 8 == s, here * 16 + rank * 4, 0)
        detail = jnp.where(lane == 126, length[s] - 256, tokens[s]).astype(F32)
        extra = jnp.where(row == s, detail, extra)
    rows = [high[:, 128 * i : 128 * i + 128] for i in range(4)]
    rows += [low[:, 128 * i : 128 * i + 128] for i in range(3)]
    rows.append(jnp.where(lane < 126, low[:, 384:], extra))
    data = jnp.concatenate(rows, axis=0).astype(BF16)
    select = jnp.where(iota((512, 64), 0) == target[0:1, 0:64], 1.0, 0.0).astype(BF16)
    return mm(select, data, NN).astype(BF16)


HALF = 768
CUT = 512
COUNT = D * 10 + 6 * D * D

SCRATCH = {
    "wave": ((SEG, D), F32),
    "w0t": ((10, 64), BF16),
    "cot": ((ROWS2, D), BF16),
    "mine0": ((64, 128), BF16),
    "send": ((32, 16, 128), BF16),
    "got": ((32, 16, 128), BF16),
    "f0": ((D, 128), BF16),
    "f1": ((D, 3 * D), BF16),
    "f2": ((D, 3 * D), BF16),
    "g0": ((D, 3 * D), BF16),
    "g1": ((D, 3 * D), BF16),
    "gf": ((D, 128), BF16),
    "rc0": ((4, 64, 3 * D), BF16),
    "rc1": ((4, 64, 3 * D), BF16),
    "rcf": ((4, 64, 128), BF16),
    "ys0": ((4, 64, 3 * D), BF16),
    "ys1": ((4, 64, 3 * D), BF16),
    "ysf": ((4, 64, 128), BF16),
    "yr0": ((4, 64, HALF), BF16),
    "yr1": ((4, 64, HALF), BF16),
    "yrf": ((4, 64, 128), BF16),
    "bx0": ((4, 4, 16, HALF), BF16),
    "bx1": ((4, 4, 16, HALF), BF16),
    "xs0": ((64, HALF), BF16),
    "xs1": ((64, HALF), BF16),
    "xsf": ((64, 128), BF16),
    "xr0": ((4, 16, HALF), BF16),
    "xr1": ((4, 16, HALF), BF16),
    "xrf": ((4, 16, 128), BF16),
    "by0": ((4, 16, HALF), BF16),
    "by1": ((4, 16, HALF), BF16),
    "bz0": ((4, 16, HALF), BF16),
    "bz1": ((4, 16, HALF), BF16),
    "zs0": ((8, 16, 256), BF16),
    "zs1": ((8, 16, 256), BF16),
    "zr0": ((8, 16, 256), BF16),
    "zr1": ((8, 16, 256), BF16),
    "fz0": ((8, 16, 256), BF16),
    "fz1": ((8, 16, 256), BF16),
    "fr0": ((4, 16, 3 * D), BF16),
    "fr1": ((4, 16, 3 * D + 128), BF16),
}
SCRATCH.update(COMPUTE_SCRATCH)
for kind in ("t", "s"):
    for axis, size in (("z", 8), ("x", 4), ("d", 8)):
        SCRATCH["all" + kind + axis] = ((size, 8, 128), F32)
        SCRATCH["my" + kind + axis] = ((8, 128), F32)

SEMS = {
    "load": 7,
    "wave": 0,
    "w0row": 4,
    "pass0": 4,
    "rowa": 8,
    "rowb": 8,
    "rowx": 32,
    "passa": 8,
    "passb": 8,
    "core": 12,
    "y": 12,
    "bx": 8,
    "x": 12,
    "by": 8,
    "z": 2,
    "fz": 2,
    "fx": 8,
    "sum": 6,
}


def whole_kernel(
    wave_in, dest_in, length_in, tokens_in, cot_in, w0_in, w1_in, w2_in,
    third_out, second_out, first_out, rms_out, dest, length, tokens, *rest,
):
    r = dict(zip(SCRATCH, rest))
    sems = rest[len(SCRATCH) :]
    sent = dict(zip(SEMS, sems[0::2]))
    came = dict(zip(SEMS, sems[1::2]))
    dp, batch, y, core, z, x = place()
    sibling = y * 2 + 1 - core

    def dp_peer(k):
        return lax.rem(dp + k, 8)

    def y_peer(k):
        return lax.rem(y + k, 4) * 2 + core

    def z_peer(k):
        return lax.rem(z + k, 8) * 4 + x

    def x_peer(k):
        return z * 4 + lax.rem(x + k, 4)

    def block(ref, who, start=0, width=3 * D):
        return ref.at[pl.ds(pl.multiple_of(who * 64, 64), 64), start : start + width]

    def quarter(ref, who, which, start, width):
        return ref.at[pl.ds(pl.multiple_of(who * 64 + which * 16, 16), 16), start : start + width]

    barrier = pltpu.get_barrier_semaphore()
    loads = [
        (wave_in, r["wave"]),
        (dest_in, dest),
        (length_in, length),
        (tokens_in, tokens),
        (cot_in, r["cot"]),
        (w0_in, r["w0t"]),
    ]
    loads = [pltpu.make_async_copy(a, b, came["load"].at[i]) for i, (a, b) in enumerate(loads)]
    full = (r["f1"], r["f2"])
    loads.append(pltpu.make_async_copy(w1_in, block(full[0], dp), came["load"].at[6]))
    loads.append(pltpu.make_async_copy(w2_in, block(full[1], dp), sent["load"].at[6]))
    for copy in loads:
        copy.start()
    loop(1, 32, lambda k: signal_to(barrier, dp, lax.rem(batch + k, 32)))
    loop(1, 8, lambda k: signal_to(barrier, dp_peer(k), batch))

    def sum_copy(kind, axis, k):
        which = 3 * (kind == "s") + "zxd".index(axis)
        mine, every = r["my" + kind + axis], r["all" + kind + axis]
        me = {"z": z, "x": x, "d": dp}[axis]
        to = {"z": (dp, z_peer(k)), "x": (dp, x_peer(k)), "d": (dp_peer(k), batch)}[axis]
        return remote(mine, every.at[me], sent["sum"].at[which], came["sum"].at[which], *to)

    def sum_start(kind, axis, value):
        size = 4 if axis == "x" else 8
        r["my" + kind + axis][...] = value
        loop(1, size, lambda k: sum_copy(kind, axis, k).start())
        r["all" + kind + axis][{"z": z, "x": x, "d": dp}[axis]] = value

    def sum_end(kind, axis):
        size = 4 if axis == "x" else 8
        every = r["all" + kind + axis]
        landed(every.at[0 : size - 1], came["sum"].at[3 * (kind == "s") + "zxd".index(axis)])
        return jnp.sum(every[...], axis=0)

    def sum_sent(kind, axis):
        size = 4 if axis == "x" else 8
        every = r["all" + kind + axis]
        landed(every.at[0 : size - 1], sent["sum"].at[3 * (kind == "s") + "zxd".index(axis)])

    for i in range(6):
        loads[i].wait()
    total = tokens[0]
    for s in range(1, SEG):
        total = total + tokens[s]
    eye = jnp.where(iota((10, 128), 0) == iota((10, 128), 1), 1.0, 0.0).astype(BF16)
    r["mine0"][...] = mm(r["w0t"][...], eye, TN).astype(BF16)
    r["send"][...] = pack_waves(r["wave"][...], dest, length, tokens).reshape(32, 16, 128)
    loads[6].wait()
    loads[7].wait()
    pl.semaphore_wait(barrier, 38)

    def wave_copy(k):
        to = lax.rem(batch + k, 32)
        return remote(r["send"].at[to], r["got"].at[batch], sent["wave"], came["wave"], dp, to)

    def w0_copy(k):
        return remote(
            r["mine0"], block(r["f0"], dp, 0, 128), sent["w0row"].at[k], came["w0row"].at[k], y_peer(k), batch
        )

    def pass0_copy(k):
        owner = y_peer(4 - k)
        here = block(r["f0"], owner, 0, 128)
        source = here if k else r["mine0"]
        return remote(source, here, sent["pass0"].at[k], came["pass0"].at[k], sibling, batch)

    def rowa_copy(w, k):
        here = block(full[w], dp, 0, CUT)
        return remote(here, here, sent["rowa"].at[w * 4 + k], came["rowa"].at[w * 4 + k], y_peer(k), batch)

    def rowb_copy(w, k):
        here = quarter(full[w], dp, x, CUT, 3 * D - CUT)
        return remote(here, here, sent["rowb"].at[w * 4 + k], came["rowb"].at[w * 4 + k], y_peer(k), batch)

    def rowx_copy(w, k, j):
        here = quarter(full[w], y_peer(4 - k), x, CUT, 3 * D - CUT)
        at = w * 16 + k * 4 + j
        return remote(here, here, sent["rowx"].at[at], came["rowx"].at[at], dp, x_peer(j))

    def passa_copy(w, k):
        here = block(full[w], y_peer(4 - k), 0, CUT)
        return remote(here, here, sent["passa"].at[w * 4 + k], came["passa"].at[w * 4 + k], sibling, batch)

    def passb_copy(w, k):
        here = block(full[w], y_peer(4 - k), CUT, 3 * D - CUT)
        return remote(here, here, sent["passb"].at[w * 4 + k], came["passb"].at[w * 4 + k], sibling, batch)

    loop(1, 32, lambda k: wave_copy(k).start())
    for k in (2, 1, 3):
        w0_copy(k).start()
    for w in range(2):
        for k in (2, 1, 3):
            rowb_copy(w, k).start()
    for w in range(2):
        for k in (2, 1, 3):
            rowa_copy(w, k).start()
    pass0_copy(0).start()
    for w in range(2):
        passa_copy(w, 0).start()
        passb_copy(w, 0).start()
    r["got"][batch] = r["send"][batch]
    block(r["f0"], dp, 0, 128)[...] = r["mine0"][...]
    sum_start("t", "z", jnp.broadcast_to(total.astype(F32), (8, 128)))
    for k in (1, 3, 2):
        w0_copy(k).wait_recv()
        pass0_copy(k).start()
    for w in range(2):
        for k in (1, 3, 2):
            rowb_copy(w, k).wait_recv()
            for j in (2, 1, 3):
                rowx_copy(w, k, j).start()

    def pass_on(w):
        for k in (1, 3, 2):
            rowa_copy(w, k).wait_recv()
            passa_copy(w, k).start()
        for k in (1, 3, 2):
            for j in (1, 3, 2):
                rowx_copy(w, k, j).wait_recv()
            passb_copy(w, k).start()

    def gathered(w):
        for k in range(4):
            passa_copy(w, k).wait_recv()
            passb_copy(w, k).wait_recv()

    landed(r["send"].at[0:31], came["wave"])
    for k in range(4):
        pass0_copy(k).wait_recv()
    forward_first(r["got"][...].reshape(512, 128), r["f0"], r)
    pass_on(0)
    sum_start("t", "x", sum_end("t", "z"))
    gathered(0)
    forward_second(full[0], r)
    pass_on(1)
    sum_start("t", "d", sum_end("t", "x"))
    gathered(1)

    def core_copy(p, k):
        step = lax.rem(y + k, 4)
        grads = r["g" + str(p)]
        width = 128 if p == "f" else 3 * D
        at = (2 if p == "f" else p) * 4 + k
        return remote(
            block(grads, step * 2 + 1 - core, 0, width), r["rc" + str(p)].at[step],
            sent["core"].at[at], came["core"].at[at], sibling, batch,
        )

    def y_copy(p, k):
        to = lax.rem(y + k, 4)
        width = 128 if p == "f" else HALF
        at = (2 if p == "f" else p) * 4 + k
        return remote(
            r["ys" + str(p)].at[to, :, 0:width], r["yr" + str(p)].at[y],
            sent["y"].at[at], came["y"].at[at], to * 2 + core, batch,
        )

    def bx_copy(p, k):
        to = lax.rem(x + k, 4)
        rows = pl.ds(pl.multiple_of(to * 16, 16), 16)
        return remote(
            r["ys" + str(p)].at[:, rows, HALF:], r["bx" + str(p)].at[x],
            sent["bx"].at[p * 4 + k], came["bx"].at[p * 4 + k], dp, z * 4 + to,
        )

    def x_copy(p, k):
        to = lax.rem(x + k, 4)
        rows = pl.ds(pl.multiple_of(to * 16, 16), 16)
        at = (2 if p == "f" else p) * 4 + k
        return remote(
            r["xs" + str(p)].at[rows], r["xr" + str(p)].at[x],
            sent["x"].at[at], came["x"].at[at], dp, z * 4 + to,
        )

    def by_copy(p, k):
        to = lax.rem(y + k, 4)
        return remote(
            r["by" + str(p)].at[to], r["bz" + str(p)].at[y],
            sent["by"].at[p * 4 + k], came["by"].at[p * 4 + k], to * 2 + core, batch,
        )

    def z_copy(p, k):
        to = lax.rem(z + k, 8)
        return remote(
            r["zs" + str(p)].at[to], r["zr" + str(p)].at[z], sent["z"].at[p], came["z"].at[p], dp, z_peer(k)
        )

    def fz_copy(p, k):
        here = r["fz" + str(p)].at[z]
        return remote(here, here, sent["fz"].at[p], came["fz"].at[p], dp, z_peer(k))

    def fx_copy(p, k):
        here = r["fr" + str(p)].at[x]
        return remote(here, here, sent["fx"].at[p * 4 + k], came["fx"].at[p * 4 + k], dp, x_peer(k))

    def core_start(p):
        for k in (2, 1, 3, 0):
            core_copy(p, k).start()

    def core_end(p):
        for k in (2, 1, 3, 0):
            step = lax.rem(y + k, 4)
            core_copy(p, k).wait_recv()
            for m in range(4):
                rows = pl.ds(pl.multiple_of((step * 2 + core) * 64 + m * 16, 16), 16)
                here = slice(m * 16, m * 16 + 16)
                own = r["g" + str(p)][rows].astype(F32)
                r["ys" + str(p)][step, here] = (own + r["rc" + str(p)][step, here].astype(F32)).astype(BF16)
            if k:
                y_copy(p, k).start()
        if p != "f":
            for k in (2, 1, 3):
                bx_copy(p, k).start()

    def y_end(p):
        width = 128 if p == "f" else HALF
        for k in (1, 3, 2):
            y_copy(p, k).wait_recv()
        for m in range(4):
            here = slice(m * 16, m * 16 + 16)
            found = r["ys" + str(p)][y, here, 0:width].astype(F32)
            for k in (1, 2, 3):
                found = found + r["yr" + str(p)][lax.rem(y + k, 4), here].astype(F32)
            r["xs" + str(p)][here] = found.astype(BF16)
        for k in (2, 1, 3):
            x_copy(p, k).start()

    def bx_end(p):
        for k in (1, 3, 2):
            bx_copy(p, k).wait_recv()
        rows = pl.ds(pl.multiple_of(x * 16, 16), 16)
        for step in range(4):
            found = r["ys" + str(p)][step, rows, HALF:].astype(F32)
            for k in (1, 2, 3):
                found = found + r["bx" + str(p)][lax.rem(x + k, 4), step].astype(F32)
            r["by" + str(p)][step] = found.astype(BF16)
        for k in (2, 1, 3):
            by_copy(p, k).start()

    def x_end(p):
        for k in (1, 3, 2):
            x_copy(p, k).wait_recv()
        found = r["xs" + str(p)][pl.ds(pl.multiple_of(x * 16, 16), 16)].astype(F32)
        for k in (1, 2, 3):
            found = found + r["xr" + str(p)][lax.rem(x + k, 4)].astype(F32)
        return found

    def by_end(p):
        for k in (1, 3, 2):
            by_copy(p, k).wait_recv()
        found = r["by" + str(p)][y].astype(F32)
        for k in (1, 2, 3):
            found = found + r["bz" + str(p)][lax.rem(y + k, 4)].astype(F32)
        return found

    def z_start(p):
        low, high = x_end(p), by_end(p)
        out = r["zs" + str(p)]
        for q in range(3):
            out[q] = low[:, q * 256 : q * 256 + 256].astype(BF16)
            out[q + 3] = high[:, q * 256 : q * 256 + 256].astype(BF16)
        out[6] = jnp.zeros((16, 256), BF16)
        out[7] = jnp.zeros((16, 256), BF16)
        if p == 1:
            out[6, :, 0:128] = x_end("f").astype(BF16)
        loop(1, 8, lambda k: z_copy(p, k).start())
        r["zr" + str(p)][z] = out[z]

    def z_end(p):
        landed(r["zr" + str(p)].at[0:7], came["z"].at[p])
        found = jnp.sum(r["zr" + str(p)][...].astype(F32), axis=0)
        r["fz" + str(p)][z] = found.astype(BF16)
        loop(1, 8, lambda k: fz_copy(p, k).start())
        return found

    def fx_start(p):
        landed(r["fz" + str(p)].at[0:7], came["fz"].at[p])
        out = r["fr" + str(p)]
        for q in range(6):
            out[x, :, q * 256 : q * 256 + 256] = r["fz" + str(p)][q]
        if p == 1:
            out[x, :, 3 * D :] = r["fz1"][6, :, 0:128]
        for k in (2, 1, 3):
            fx_copy(p, k).start()

    third_layer(r["cot"], full[1], r)
    grad_third(r["g0"], r)
    core_start(0)
    back_second(full[1], r)
    core_end(0)
    grad_second(r["g1"], r)
    core_start(1)
    back_first(full[0], r)
    core_end(1)
    grad_first(r["gf"], r)
    core_start("f")
    y_end(0)
    bx_end(0)
    core_end("f")
    token_sum = sum_end("t", "d")
    per_token = (1.0 / token_sum)[0:1, 0:1]
    z_start(0)
    y_end(1)
    bx_end(1)
    y_end("f")
    found = z_end(0) * per_token
    squares = jnp.sum(found * found, keepdims=True)
    z_start(1)
    fx_start(0)
    found = z_end(1) * per_token
    squares = squares + jnp.sum(found * found, keepdims=True)
    sum_start("s", "z", jnp.broadcast_to(squares, (8, 128)))
    fx_start(1)
    sum_start("s", "x", sum_end("s", "z"))
    sum_start("s", "d", sum_end("s", "x"))
    rms = jnp.sqrt(sum_end("s", "d") * (1.0 / COUNT))
    factor = (1.0 / (token_sum * jnp.maximum(rms, 1.0)))[0:1, 0:1]
    for k in (1, 3, 2):
        fx_copy(0, k).wait_recv()
    third_out[...] = r["fr0"][...].reshape(64, 3 * D).astype(F32) * factor
    for k in (1, 3, 2):
        fx_copy(1, k).wait_recv()
    second_out[...] = r["fr1"][:, :, 0 : 3 * D].reshape(64, 3 * D).astype(F32) * factor
    first = r["fr1"][:, :, 3 * D :].reshape(64, 128).astype(F32) * factor
    square = jnp.concatenate([first, jnp.zeros((64, 128), F32)], axis=0)
    first_out[...] = square.T[0:10, 0:64]
    rms_out[...] = rms

    landed(r["send"].at[0:31], sent["wave"])
    for k in range(4):
        pass0_copy(k).wait_send()
        if k:
            w0_copy(k).wait_send()
        for w in range(2):
            passa_copy(w, k).wait_send()
            passb_copy(w, k).wait_send()
            if k:
                rowa_copy(w, k).wait_send()
                rowb_copy(w, k).wait_send()
                for j in range(1, 4):
                    rowx_copy(w, k, j).wait_send()
        for p in (0, 1, "f"):
            core_copy(p, k).wait_send()
            if k:
                y_copy(p, k).wait_send()
                x_copy(p, k).wait_send()
                if p != "f":
                    bx_copy(p, k).wait_send()
                    by_copy(p, k).wait_send()
                    fx_copy(p, k).wait_send()
    for p in range(2):
        landed(r["zr" + str(p)].at[0:7], sent["z"].at[p])
        landed(r["fz" + str(p)].at[0:7], sent["fz"].at[p])
    for kind in "ts":
        for axis in "zxd":
            sum_sent(kind, axis)


def whole(wave, dest, length, tokens, cot, w0, w1, w2):
    vmem = pl.BlockSpec(memory_space=pltpu.VMEM)
    anywhere = pl.BlockSpec(memory_space=pl.ANY)
    sems = []
    for count in SEMS.values():
        sems += [pltpu.SemaphoreType.DMA((count,)) if count else pltpu.SemaphoreType.DMA] * 2
    return pl.pallas_call(
        whole_kernel,
        out_shape=(
            jax.ShapeDtypeStruct((64, 3 * D), F32),
            jax.ShapeDtypeStruct((64, 3 * D), F32),
            jax.ShapeDtypeStruct((10, 64), F32),
            jax.ShapeDtypeStruct((8, 128), F32),
        ),
        in_specs=[anywhere] * 8,
        out_specs=(vmem,) * 4,
        scratch_shapes=[pltpu.SMEM((SEG,), jnp.int32)] * 3
        + [pltpu.VMEM(s, t) for s, t in SCRATCH.values()]
        + sems,
        compiler_params=pltpu.CompilerParams(
            collective_id=0, has_side_effects=True, vmem_limit_bytes=58 << 20
        ),
        cost_estimate=pl.CostEstimate(flops=3000000000, bytes_accessed=3000000, transcendentals=1400000),
    )(wave, dest, length, tokens, cot, w0, w1, w2)


def local(wave, length, dest, tokens, cot, w0, w1, w2):
    third, second, first, rms = whole(
        wave, dest, length, tokens, cot.reshape(ROWS2, D), w0.T, w1, w2
    )
    return first.T, second, third, rms[0, 0:1]


def solution(mesh):
    row = P(("dp", "batch"))
    return jax.shard_map(
        local,
        mesh=mesh,
        in_specs=(row, row, row, row, row, P("dp"), P("dp"), P("dp")),
        out_specs=(P("dp"), P("dp"), P("dp"), P()),
        check_vma=False,
    )
```

time: 137 us -> 75.8 us (0.55)
  Pallas kernels: 123 us -> 70.6 us
  local copies, waits for them, and re-layouts: 13.1 us -> 4.36 us
    pallas_call x3 -> x1, Pallas kernels: 123 us -> 70.6 us  [whole(): pl.pallas_call(whole_kernel, out_shape=(jax.ShapeDtypeStruct((64, 3 * D),...]
    unnamed x26 -> x7, local copies, waits for them, and re-layouts: 11.6 us -> 3.17 us
where the time goes in v2:
time: 75.8 us; the launch traced here: 75.6 us
  Pallas kernels  70.6 us (93%)
  local copies, waits for them, and re-layouts  4.36 us (6%)
    pallas_call x1, Pallas kernels, whole(): pl.pallas_call(whole_kernel, out_shape=(jax.ShapeDtypeStruct((64, 3 * D),...  70.6 us
    unnamed x7, local copies, waits for them, and re-layouts  3.17 us

profile of v2, /device:TPU:1, one launch (start us, length us, event | category | flops | bytes accessed | tf_op | source)
XLA Modules:
  0.0 75.6 jit_solution(1022249997602496769)
XLA Ops:
  0.6 70.6 %shard_map.111 = (f32[64,1536]{1,0:T(8,128)}, f32[64,1536]{1,0:T(8,128)}, f32[10,64]{1,0:T(8,128)}, f32[8,128]{1,0:T(8,128)}) custom-call(f32[8,512]{1,0:T(8,128)} %wave_in.1, s32[8]{0:T(128)} %dest_in.1, s32[8]{0:T(128)} %length_in.1, s32[8]{0:T(128)} %tokens_in.1, bf16[192,512]{1,0:T(8,128)(2,1)} %bitcast.5, bf16[10,64]{1,0:T(8,128)(2,1)} %bitcast.6, ...), custom_call_target="tpu_custom_call" | custom-call | flops 3000000000 | bytes 3000000 | tf_op jit(solution)/shard_map/pallas_call | solution.py:821
  71.2 0.0 copy-start.1
  71.2 1.2 %slice.3 = f32[1,1]{1,0:T(1,128)} slice(f32[8,128]{1,0:T(8,128)} %get-tuple-element.11), slice={[0:1], [0:1]} | slice | bytes 8 | tf_op jit(solution)/shard_map/slice | solution.py:845
  72.4 0.0 copy-done.1
  72.4 0.6 copy.15
  73.0 0.0 copy-start
  73.0 1.8 %copy.16 = f32[64,1536]{1,0:T(8,128)} copy(f32[64,1536]{1,0:T(8,128)} %get-tuple-element.17) | data formatting | bytes 786432
  74.8 0.0 copy-done
  74.8 0.7 copy.17
Async XLA Ops:
  71.2 1.2 %copy-start.1 = (f32[10,64]{1,0:T(8,128)S(1)}, f32[10,64]{1,0:T(8,128)}, u32[]{:S(2)}) copy-start(f32[10,64]{1,0:T(8,128)} %get-tuple-element.8) | copy-start | bytes 7684
  73.0 1.8 %copy-start = (f32[64,1536]{1,0:T(8,128)S(1)}, f32[64,1536]{1,0:T(8,128)}, u32[]{:S(2)}) copy-start(f32[64,1536]{1,0:T(8,128)} %get-tuple-element.18) | copy-start | bytes 1179652

commit v3 on v2

--- a/solution.py
+++ b/solution.py
@@ -204,8 +204,8 @@
     lax.fori_loop(0, ROWS2 // 16, body, 0, unroll=UNROLL)
 
 
-def grad_third(out_ref, r):
-    out_ref[...] = mm(r["d2"][...], r["p2"][0:ROWS2], TN).astype(out_ref.dtype)
+def grad_third(rows, r):
+    r["g0"][rows] = mm(r["d2"][:, rows], r["p2"][0:ROWS2], TN).astype(BF16)
 
 
 def back_second(w2_ref, r):
@@ -234,8 +234,8 @@
     lax.fori_loop(0, ROWS // 16, odd, 0, unroll=UNROLL)
 
 
-def grad_second(out_ref, r):
-    out_ref[...] = mm(r["d1"][...], r["p1"][...], TN).astype(out_ref.dtype)
+def grad_second(rows, r):
+    r["g1"][rows] = mm(r["d1"][:, rows], r["p1"][...], TN).astype(BF16)
 
 
 def back_first(w1_ref, r):
@@ -348,7 +348,7 @@
 
 
 HALF = 768
-CUT = 512
+CUT = 768
 COUNT = D * 10 + 6 * D * D
 
 SCRATCH = {
@@ -391,13 +391,11 @@
     "zr1": ((8, 16, 256), BF16),
     "fz0": ((8, 16, 256), BF16),
     "fz1": ((8, 16, 256), BF16),
-    "fr0": ((4, 16, 3 * D), BF16),
-    "fr1": ((4, 16, 3 * D + 128), BF16),
 }
 SCRATCH.update(COMPUTE_SCRATCH)
 for kind in ("t", "s"):
-    for axis, size in (("z", 8), ("x", 4), ("d", 8)):
-        SCRATCH["all" + kind + axis] = ((size, 8, 128), F32)
+    for axis in "zg":
+        SCRATCH["all" + kind + axis] = ((16, 8, 128), F32)
         SCRATCH["my" + kind + axis] = ((8, 128), F32)
 
 SEMS = {
@@ -418,23 +416,30 @@
     "z": 2,
     "fz": 2,
     "fx": 8,
-    "sum": 6,
+    "sum": 4,
 }
 
 
 def whole_kernel(
     wave_in, dest_in, length_in, tokens_in, cot_in, w0_in, w1_in, w2_in,
-    third_out, second_out, first_out, rms_out, dest, length, tokens, *rest,
+    third_out, second_out, stat_out, dest, length, tokens, *rest,
 ):
-    r = dict(zip(SCRATCH, rest))
+    r = dict(zip(SCRATCH, rest), fr0=third_out, fr1=second_out)
     sems = rest[len(SCRATCH) :]
     sent = dict(zip(SEMS, sems[0::2]))
     came = dict(zip(SEMS, sems[1::2]))
     dp, batch, y, core, z, x = place()
     sibling = y * 2 + 1 - core
 
-    def dp_peer(k):
-        return lax.rem(dp + k, 8)
+    column, plane = z * 2 + core, y * 4 + x
+
+    def column_peer(k):
+        other = lax.rem(column + k, 16)
+        return y * 2 + other % 2, other // 2 * 4 + x
+
+    def plane_peer(k):
+        other = lax.rem(plane + k, 16)
+        return other // 4 * 2 + core, z * 4 + other % 4
 
     def y_peer(k):
         return lax.rem(y + k, 4) * 2 + core
@@ -467,90 +472,90 @@
     for copy in loads:
         copy.start()
     loop(1, 32, lambda k: signal_to(barrier, dp, lax.rem(batch + k, 32)))
-    loop(1, 8, lambda k: signal_to(barrier, dp_peer(k), batch))
+    loop(0, 8, lambda k: signal_to(barrier, sibling, z_peer(k)))
+    loop(4, 16, lambda k: signal_to(barrier, lax.rem(y + k // 4, 4) * 2 + core, z * 4 + k % 4))
 
     def sum_copy(kind, axis, k):
-        which = 3 * (kind == "s") + "zxd".index(axis)
+        which = 2 * (kind == "s") + (axis == "g")
         mine, every = r["my" + kind + axis], r["all" + kind + axis]
-        me = {"z": z, "x": x, "d": dp}[axis]
-        to = {"z": (dp, z_peer(k)), "x": (dp, x_peer(k)), "d": (dp_peer(k), batch)}[axis]
+        if axis == "z":
+            me, to = column, column_peer(k)
+        else:
+            me, to = plane, plane_peer(k)
         return remote(mine, every.at[me], sent["sum"].at[which], came["sum"].at[which], *to)
 
     def sum_start(kind, axis, value):
-        size = 4 if axis == "x" else 8
         r["my" + kind + axis][...] = value
-        loop(1, size, lambda k: sum_copy(kind, axis, k).start())
-        r["all" + kind + axis][{"z": z, "x": x, "d": dp}[axis]] = value
+        loop(1, 16, lambda k: sum_copy(kind, axis, k).start())
+        r["all" + kind + axis][column if axis == "z" else plane] = value
 
     def sum_end(kind, axis):
-        size = 4 if axis == "x" else 8
         every = r["all" + kind + axis]
-        landed(every.at[0 : size - 1], came["sum"].at[3 * (kind == "s") + "zxd".index(axis)])
+        landed(every.at[0:15], came["sum"].at[2 * (kind == "s") + (axis == "g")])
         return jnp.sum(every[...], axis=0)
 
     def sum_sent(kind, axis):
-        size = 4 if axis == "x" else 8
         every = r["all" + kind + axis]
-        landed(every.at[0 : size - 1], sent["sum"].at[3 * (kind == "s") + "zxd".index(axis)])
-
+        landed(every.at[0:15], sent["sum"].at[2 * (kind == "s") + (axis == "g")])
+
+    def wave_copy(k):
+        to = lax.rem(batch + k, 32)
+        return remote(r["send"].at[to], r["got"].at[batch], sent["wave"], came["wave"], dp, to)
+
+    def w0_copy(k):
+        return remote(
+            r["mine0"], block(r["f0"], dp, 0, 128), sent["w0row"].at[k], came["w0row"].at[k], y_peer(k), batch
+        )
+
+    def pass0_copy(k):
+        owner = y_peer(4 - k)
+        here = block(r["f0"], owner, 0, 128)
+        source = here if k else r["mine0"]
+        return remote(source, here, sent["pass0"].at[k], came["pass0"].at[k], sibling, batch)
+
+    def rowa_copy(w, k):
+        here = block(full[w], dp, 0, CUT)
+        return remote(here, here, sent["rowa"].at[w * 4 + k], came["rowa"].at[w * 4 + k], y_peer(k), batch)
+
+    def rowb_copy(w, k):
+        here = quarter(full[w], dp, x, CUT, 3 * D - CUT)
+        return remote(here, here, sent["rowb"].at[w * 4 + k], came["rowb"].at[w * 4 + k], y_peer(k), batch)
+
+    def rowx_copy(w, k, j):
+        here = quarter(full[w], y_peer(4 - k), x, CUT, 3 * D - CUT)
+        at = w * 16 + k * 4 + j
+        return remote(here, here, sent["rowx"].at[at], came["rowx"].at[at], dp, x_peer(j))
+
+    def passa_copy(w, k):
+        here = block(full[w], y_peer(4 - k), 0, CUT)
+        return remote(here, here, sent["passa"].at[w * 4 + k], came["passa"].at[w * 4 + k], sibling, batch)
+
+    def passb_copy(w, k):
+        here = block(full[w], y_peer(4 - k), CUT, 3 * D - CUT)
+        return remote(here, here, sent["passb"].at[w * 4 + k], came["passb"].at[w * 4 + k], sibling, batch)
+
+    loads[6].wait()
+    loads[7].wait()
+    pl.semaphore_wait(barrier, 51)
+    for w in range(2):
+        for k in (2, 1, 3):
+            rowb_copy(w, k).start()
     for i in range(6):
-        loads[i].wait()
+        if i != 4:
+            loads[i].wait()
     total = tokens[0]
     for s in range(1, SEG):
         total = total + tokens[s]
     eye = jnp.where(iota((10, 128), 0) == iota((10, 128), 1), 1.0, 0.0).astype(BF16)
     r["mine0"][...] = mm(r["w0t"][...], eye, TN).astype(BF16)
-    r["send"][...] = pack_waves(r["wave"][...], dest, length, tokens).reshape(32, 16, 128)
-    loads[6].wait()
-    loads[7].wait()
-    pl.semaphore_wait(barrier, 38)
-
-    def wave_copy(k):
-        to = lax.rem(batch + k, 32)
-        return remote(r["send"].at[to], r["got"].at[batch], sent["wave"], came["wave"], dp, to)
-
-    def w0_copy(k):
-        return remote(
-            r["mine0"], block(r["f0"], dp, 0, 128), sent["w0row"].at[k], came["w0row"].at[k], y_peer(k), batch
-        )
-
-    def pass0_copy(k):
-        owner = y_peer(4 - k)
-        here = block(r["f0"], owner, 0, 128)
-        source = here if k else r["mine0"]
-        return remote(source, here, sent["pass0"].at[k], came["pass0"].at[k], sibling, batch)
-
-    def rowa_copy(w, k):
-        here = block(full[w], dp, 0, CUT)
-        return remote(here, here, sent["rowa"].at[w * 4 + k], came["rowa"].at[w * 4 + k], y_peer(k), batch)
-
-    def rowb_copy(w, k):
-        here = quarter(full[w], dp, x, CUT, 3 * D - CUT)
-        return remote(here, here, sent["rowb"].at[w * 4 + k], came["rowb"].at[w * 4 + k], y_peer(k), batch)
-
-    def rowx_copy(w, k, j):
-        here = quarter(full[w], y_peer(4 - k), x, CUT, 3 * D - CUT)
-        at = w * 16 + k * 4 + j
-        return remote(here, here, sent["rowx"].at[at], came["rowx"].at[at], dp, x_peer(j))
-
-    def passa_copy(w, k):
-        here = block(full[w], y_peer(4 - k), 0, CUT)
-        return remote(here, here, sent["passa"].at[w * 4 + k], came["passa"].at[w * 4 + k], sibling, batch)
-
-    def passb_copy(w, k):
-        here = block(full[w], y_peer(4 - k), CUT, 3 * D - CUT)
-        return remote(here, here, sent["passb"].at[w * 4 + k], came["passb"].at[w * 4 + k], sibling, batch)
-
-    loop(1, 32, lambda k: wave_copy(k).start())
     for k in (2, 1, 3):
         w0_copy(k).start()
-    for w in range(2):
-        for k in (2, 1, 3):
-            rowb_copy(w, k).start()
+    pass0_copy(0).start()
+    r["send"][...] = pack_waves(r["wave"][...], dest, length, tokens).reshape(32, 16, 128)
+    loop(11, 42, lambda k: wave_copy(1 + lax.rem(k, 31)).start())
     for w in range(2):
         for k in (2, 1, 3):
             rowa_copy(w, k).start()
-    pass0_copy(0).start()
     for w in range(2):
         passa_copy(w, 0).start()
         passb_copy(w, 0).start()
@@ -585,11 +590,10 @@
         pass0_copy(k).wait_recv()
     forward_first(r["got"][...].reshape(512, 128), r["f0"], r)
     pass_on(0)
-    sum_start("t", "x", sum_end("t", "z"))
+    sum_start("t", "g", sum_end("t", "z"))
     gathered(0)
     forward_second(full[0], r)
     pass_on(1)
-    sum_start("t", "d", sum_end("t", "x"))
     gathered(1)
 
     def core_copy(p, k):
@@ -649,8 +653,10 @@
         here = r["fr" + str(p)].at[x]
         return remote(here, here, sent["fx"].at[p * 4 + k], came["fx"].at[p * 4 + k], dp, x_peer(k))
 
-    def core_start(p):
+    def core_start(p, grad=None):
         for k in (2, 1, 3, 0):
+            if grad is not None:
+                grad(pl.ds(pl.multiple_of(lax.rem(y + k, 4) * 128, 128), 128), r)
             core_copy(p, k).start()
 
     def core_end(p):
@@ -722,12 +728,16 @@
         loop(1, 8, lambda k: z_copy(p, k).start())
         r["zr" + str(p)][z] = out[z]
 
-    def z_end(p):
+    def z_end(p, per_token, other=None):
         landed(r["zr" + str(p)].at[0:7], came["z"].at[p])
         found = jnp.sum(r["zr" + str(p)][...].astype(F32), axis=0)
         r["fz" + str(p)][z] = found.astype(BF16)
+        found = found * per_token
+        squares = jnp.sum(found * found, keepdims=True)
+        if p == 1:
+            sum_start("s", "z", jnp.broadcast_to(squares + other, (8, 128)))
         loop(1, 8, lambda k: fz_copy(p, k).start())
-        return found
+        return squares
 
     def fx_start(p):
         landed(r["fz" + str(p)].at[0:7], came["fz"].at[p])
@@ -739,48 +749,38 @@
         for k in (2, 1, 3):
             fx_copy(p, k).start()
 
+    loads[4].wait()
     third_layer(r["cot"], full[1], r)
-    grad_third(r["g0"], r)
-    core_start(0)
+    core_start(0, grad_third)
     back_second(full[1], r)
     core_end(0)
-    grad_second(r["g1"], r)
-    core_start(1)
+    core_start(1, grad_second)
     back_first(full[0], r)
     core_end(1)
     grad_first(r["gf"], r)
     core_start("f")
+    core_end("f")
     y_end(0)
     bx_end(0)
-    core_end("f")
-    token_sum = sum_end("t", "d")
+    token_sum = sum_end("t", "g")
     per_token = (1.0 / token_sum)[0:1, 0:1]
     z_start(0)
     y_end(1)
     bx_end(1)
     y_end("f")
-    found = z_end(0) * per_token
-    squares = jnp.sum(found * found, keepdims=True)
     z_start(1)
+    squares = z_end(0, per_token)
     fx_start(0)
-    found = z_end(1) * per_token
-    squares = squares + jnp.sum(found * found, keepdims=True)
-    sum_start("s", "z", jnp.broadcast_to(squares, (8, 128)))
+    z_end(1, per_token, squares)
     fx_start(1)
-    sum_start("s", "x", sum_end("s", "z"))
-    sum_start("s", "d", sum_end("s", "x"))
-    rms = jnp.sqrt(sum_end("s", "d") * (1.0 / COUNT))
+    sum_start("s", "g", sum_end("s", "z"))
+    rms = jnp.sqrt(sum_end("s", "g") * (1.0 / COUNT))
     factor = (1.0 / (token_sum * jnp.maximum(rms, 1.0)))[0:1, 0:1]
-    for k in (1, 3, 2):
-        fx_copy(0, k).wait_recv()
-    third_out[...] = r["fr0"][...].reshape(64, 3 * D).astype(F32) * factor
-    for k in (1, 3, 2):
-        fx_copy(1, k).wait_recv()
-    second_out[...] = r["fr1"][:, :, 0 : 3 * D].reshape(64, 3 * D).astype(F32) * factor
-    first = r["fr1"][:, :, 3 * D :].reshape(64, 128).astype(F32) * factor
-    square = jnp.concatenate([first, jnp.zeros((64, 128), F32)], axis=0)
-    first_out[...] = square.T[0:10, 0:64]
-    rms_out[...] = rms
+    stat_out[0:8] = jnp.broadcast_to(factor, (8, 128))
+    stat_out[8:16] = rms
+    for p in range(2):
+        for k in (1, 3, 2):
+            fx_copy(p, k).wait_recv()
 
     landed(r["send"].at[0:31], sent["wave"])
     for k in range(4):
@@ -808,7 +808,7 @@
         landed(r["zr" + str(p)].at[0:7], sent["z"].at[p])
         landed(r["fz" + str(p)].at[0:7], sent["fz"].at[p])
     for kind in "ts":
-        for axis in "zxd":
+        for axis in "zg":
             sum_sent(kind, axis)
 
 
@@ -821,13 +821,12 @@
     return pl.pallas_call(
         whole_kernel,
         out_shape=(
-            jax.ShapeDtypeStruct((64, 3 * D), F32),
-            jax.ShapeDtypeStruct((64, 3 * D), F32),
-            jax.ShapeDtypeStruct((10, 64), F32),
-            jax.ShapeDtypeStruct((8, 128), F32),
+            jax.ShapeDtypeStruct((4, 16, 3 * D), BF16),
+            jax.ShapeDtypeStruct((4, 16, 3 * D + 128), BF16),
+            jax.ShapeDtypeStruct((16, 128), F32),
         ),
         in_specs=[anywhere] * 8,
-        out_specs=(vmem,) * 4,
+        out_specs=(vmem,) * 3,
         scratch_shapes=[pltpu.SMEM((SEG,), jnp.int32)] * 3
         + [pltpu.VMEM(s, t) for s, t in SCRATCH.values()]
         + sems,
@@ -838,11 +837,32 @@
     )(wave, dest, length, tokens, cot, w0, w1, w2)
 
 
+def scale_kernel(third, second, stat, third_out, second_out, first_out, rms_out):
+    factor = stat[0:1, 0:1]
+    third_out[...] = third[...].astype(F32) * factor
+    second_out[...] = second[:, 0 : 3 * D].astype(F32) * factor
+    first = second[:, 3 * D :].astype(F32) * factor
+    square = jnp.concatenate([first, jnp.zeros((64, 128), F32)], axis=0)
+    first_out[...] = square.T[0:10, 0:64]
+    rms_out[0] = jnp.max(stat[8:16])
+
+
 def local(wave, length, dest, tokens, cot, w0, w1, w2):
-    third, second, first, rms = whole(
-        wave, dest, length, tokens, cot.reshape(ROWS2, D), w0.T, w1, w2
-    )
-    return first.T, second, third, rms[0, 0:1]
+    third, second, stat = whole(wave, dest, length, tokens, cot.reshape(ROWS2, D), w0.T, w1, w2)
+    vmem = pl.BlockSpec(memory_space=pltpu.VMEM)
+    third, second, first, rms = pl.pallas_call(
+        scale_kernel,
+        out_shape=(
+            jax.ShapeDtypeStruct((64, 3 * D), F32),
+            jax.ShapeDtypeStruct((64, 3 * D), F32),
+            jax.ShapeDtypeStruct((10, 64), F32),
+            jax.ShapeDtypeStruct((1,), F32),
+        ),
+        in_specs=[vmem] * 3,
+        out_specs=(vmem, vmem, vmem, pl.BlockSpec(memory_space=pltpu.SMEM)),
+        compiler_params=pltpu.CompilerParams(vmem_limit_bytes=16 << 20),
+    )(third.reshape(64, 3 * D), second.reshape(64, 3 * D + 128), stat)
+    return first.T, second, third, rms
 
 
 def solution(mesh):

time: 75.8 us -> 71.3 us (0.941); the launches traced: 75.6 us -> 70.3 us
  Pallas kernels: 70.6 us -> 67.1 us
  local copies, waits for them, and re-layouts: 4.36 us -> 2.55 us
    pallas_call x1 -> x2, Pallas kernels: 70.6 us -> 67.1 us  [the longest x1 66.2 us: whole(): pl.pallas_call(whole_kernel, out_shape=(jax.ShapeDtypeStruct((4, 16, 3 *...]
    slice x1 -> x0, local copies, waits for them, and re-layouts: 1.19 us -> none  [local(): return (first.T, second, third, rms[0, 0:1])]
    unnamed x7 -> x6, local copies, waits for them, and re-layouts: 3.17 us -> 2.55 us
where the time goes in v3:
time: 71.3 us; the launch traced here: 70.3 us
  Pallas kernels  67.1 us (94%)
  local copies, waits for them, and re-layouts  2.55 us (4%)
    pallas_call x1, Pallas kernels, whole(): pl.pallas_call(whole_kernel, out_shape=(jax.ShapeDtypeStruct((4, 16, 3 *...  66.2 us
    unnamed x6, local copies, waits for them, and re-layouts  2.55 us

profile of v3, /device:TPU:1, one launch (start us, length us, event | category | flops | bytes accessed | tf_op | source)
XLA Modules:
  0.0 70.3 jit_solution(13361741180190431054)
XLA Ops:
  0.6 66.2 %shard_map.111 = (bf16[4,16,1536]{2,1,0:T(8,128)(2,1)}, bf16[4,16,1664]{2,1,0:T(8,128)(2,1)}, f32[16,128]{1,0:T(8,128)}) custom-call(f32[8,512]{1,0:T(8,128)} %wave_in.1, s32[8]{0:T(128)} %dest_in.1, s32[8]{0:T(128)} %length_in.1, s32[8]{0:T(128)} %tokens_in.1, bf16[192,512]{1,0:T(8,128)(2,1)} %bitcast.7, bf16[10,64]{1,0:T(8,128)(2,1)} %bitcast.9, ...), custom_call_target="tpu_custom_call" | custom-call | flops 3000000000 | bytes 3000000 | tf_op jit(solution)/shard_map/pallas_call | solution.py:821
  66.8 0.0 copy-start.2
  66.8 0.7 copy-done.2
  67.5 0.0 copy-start
  67.5 0.9 %copy-done = bf16[4,16,1664]{2,1,0:T(8,128)(2,1)S(1)} copy-done((bf16[4,16,1664]{2,1,0:T(8,128)(2,1)S(1)}, bf16[4,16,1664]{2,1,0:T(8,128)(2,1)}, u32[]{:S(2)}) %copy-start) | copy-done | bytes 213016
  68.4 0.0 copy-start.1
  68.4 0.9 %copy-done.1 = bf16[4,16,1536]{2,1,0:T(8,128)(2,1)S(1)} copy-done((bf16[4,16,1536]{2,1,0:T(8,128)(2,1)S(1)}, bf16[4,16,1536]{2,1,0:T(8,128)(2,1)}, u32[]{:S(2)}) %copy-start.1) | copy-done | bytes 196632
  69.4 0.9 %shard_map.112 = (f32[64,1536]{1,0:T(8,128)}, f32[64,1536]{1,0:T(8,128)}, f32[10,64]{1,0:T(8,128)}, f32[1]{0:T(128)}) custom-call(bf16[64,1536]{1,0:T(8,128)(2,1)S(1)} %bitcast.6, bf16[64,1664]{1,0:T(8,128)(2,1)S(1)} %bitcast.5, f32[16,128]{1,0:T(8,128)S(1)} %copy-done.2), custom_call_target="tpu_custom_call" | custom-call | tf_op jit(solution)/shard_map/pallas_call | solution.py:853
Async XLA Ops:
  66.8 0.7 copy-start.2
  67.5 0.9 %copy-start = (bf16[4,16,1664]{2,1,0:T(8,128)(2,1)S(1)}, bf16[4,16,1664]{2,1,0:T(8,128)(2,1)}, u32[]{:S(2)}) copy-start(bf16[4,16,1664]{2,1,0:T(8,128)(2,1)} %get-tuple-element.12) | copy-start | bytes 638980
  68.4 0.9 %copy-start.1 = (bf16[4,16,1536]{2,1,0:T(8,128)(2,1)S(1)}, bf16[4,16,1536]{2,1,0:T(8,128)(2,1)}, u32[]{:S(2)}) copy-start(bf16[4,16,1536]{2,1,0:T(8,128)(2,1)} %get-tuple-element.11) | copy-start | bytes 589828

commit v4 on v3

--- a/solution.py
+++ b/solution.py
@@ -46,12 +46,7 @@
     return inverse * (grad - mean(grad) - normed * mean(grad * normed))
 
 
-def pick_waves(got):
-    lane_pick = (iota((SEG, 128), 1) == 127).astype(BF16)
-    token_row = mm(lane_pick, got, NT)
-    column = iota((SEG, 512), 1)
-    carries = jnp.logical_and(column % 16 >= 8, column % 4 == 3)
-    filled = jnp.where(jnp.logical_and(carries, token_row > 0.5), 1.0, 0.0).astype(BF16)
+def rank_weights():
     row_slot = iota((512, 512), 0)
     row_slot = (row_slot // 16) * 2 + (row_slot // 4) % 2
     column_slot = iota((512, 512), 1)
@@ -59,7 +54,16 @@
     weight = jnp.where(row_slot < column_slot, 1.0, 0.0) + jnp.where(
         row_slot == column_slot, 64.0, 0.0
     )
-    place = mm(filled, weight.astype(BF16), NN) - 64.0
+    return weight.astype(BF16)
+
+
+def pick_waves(got, ranks):
+    lane_pick = (iota((SEG, 128), 1) == 127).astype(BF16)
+    token_row = mm(lane_pick, got, NT)
+    column = iota((SEG, 512), 1)
+    carries = jnp.logical_and(column % 16 >= 8, column % 4 == 3)
+    filled = jnp.where(jnp.logical_and(carries, token_row > 0.5), 1.0, 0.0).astype(BF16)
+    place = mm(filled, ranks, NN) - 64.0
     target = place + ((column // 8) % 2 * 32 + (column % 4) * 8).astype(F32)
     target = jnp.where(place > -0.5, target, -1.0)
     picking = jnp.where(iota((64, 512), 0).astype(F32) == target[0:1], 1.0, 0.0).astype(BF16)
@@ -91,8 +95,23 @@
     return jnp.where(iota((ROWS, 128), 1) < 32, taps, 0.0)
 
 
-def forward_first(got, w0_ref, r):
-    wave, length, tokens = pick_waves(got)
+def before_waves(r):
+    r["ranks"][...] = rank_weights()
+    row, column = iota((ROWS2, ROWS2), 0), iota((ROWS2, ROWS2), 1)
+    order = jnp.where(column == (row % SEG) * F2 + row // SEG, 1.0, 0.0).astype(BF16)
+    r["c2"][...] = mm(order, r["cot"][...], NN)
+
+
+def spread_first(w0, r):
+    tap_row, tap_column = iota((128, 128), 0), iota((128, 128), 1)
+    for c in range(4):
+        placing = jnp.logical_and(tap_row % 32 == tap_column + 5 * c, tap_row < 64)
+        placing = jnp.logical_and(placing, tap_column < 10)
+        r["w0x"][c] = mm(jnp.where(placing, 1.0, 0.0).astype(BF16), w0, NT).astype(BF16)
+
+
+def forward_first(got, r):
+    wave, length, tokens = pick_waves(got, r["ranks"][...])
     taps = first_taps(wave, length)
     high = taps.astype(BF16).astype(F32)
     both = high + pltpu.roll(taps - high, 32, axis=1)
@@ -103,13 +122,8 @@
         keep = narrow_lane % 32 < 10
         moved = jnp.where(jnp.logical_and(keep, narrow_lane < 64), moved, 0.0)
         r["x4"][c * ROWS : (c + 1) * ROWS] = moved.astype(BF16)
-    w0 = w0_ref[...]
-    tap_row, tap_column = iota((128, 128), 0), iota((128, 128), 1)
     for c in range(4):
-        placing = jnp.logical_and(tap_row % 32 == tap_column + 5 * c, tap_row < 64)
-        placing = jnp.logical_and(placing, tap_column < 10)
-        weight = mm(jnp.where(placing, 1.0, 0.0).astype(BF16), w0, NT).astype(BF16)
-        r["z0"][c * ROWS : (c + 1) * ROWS] = mm(both_narrow, weight, NN)
+        r["z0"][c * ROWS : (c + 1) * ROWS] = mm(both_narrow, r["w0x"][c], NN)
     l2 = ((((length - 10.0) * 0.2).astype(jnp.int32) + 1 - 3) // 2 + 1 - 3) // 2 + 1
     r["info"][0:8] = jnp.broadcast_to(l2.astype(F32), (SEG, 128))
     r["info"][8:16] = jnp.broadcast_to(tokens, (SEG, 128))
@@ -183,11 +197,8 @@
     lax.fori_loop(0, ROWS // 16, spread, 0, unroll=UNROLL)
 
 
-def third_layer(cot_ref, w2_ref, r):
+def third_layer(w2_ref, r):
     r["z2"][...] = mm(r["p2"][0:ROWS2], w2_ref[...], NT)
-    row, column = iota((ROWS2, ROWS2), 0), iota((ROWS2, ROWS2), 1)
-    order = jnp.where(column == (row % SEG) * F2 + row // SEG, 1.0, 0.0).astype(BF16)
-    r["c2"][...] = mm(order, cot_ref[...], NN)
     limit = jnp.concatenate([r["info"][0:8, 0:1]] * 2, axis=0)
     tokens = jnp.concatenate([r["info"][8:16, 0:1]] * 2, axis=0)
     half = (iota((16, 1), 0) // 8).astype(F32)
@@ -271,6 +282,8 @@
 
 
 COMPUTE_SCRATCH = {
+    "ranks": ((512, 512), BF16),
+    "w0x": ((4, 128, D), BF16),
     "x4": ((4 * ROWS, 128), BF16),
     "z0": ((4 * ROWS, D), F32),
     "s0": ((4 * ROWS, D), F32),
@@ -392,6 +405,9 @@
     "fz0": ((8, 16, 256), BF16),
     "fz1": ((8, 16, 256), BF16),
 }
+SCRATCH["fr0"] = ((4, 16, 3 * D), BF16)
+SCRATCH["fr1"] = ((4, 16, 3 * D + 128), BF16)
+SCRATCH["stat"] = ((16, 128), F32)
 SCRATCH.update(COMPUTE_SCRATCH)
 for kind in ("t", "s"):
     for axis in "zg":
@@ -417,6 +433,7 @@
     "fz": 2,
     "fx": 8,
     "sum": 4,
+    "out": 3,
 }
 
 
@@ -424,7 +441,7 @@
     wave_in, dest_in, length_in, tokens_in, cot_in, w0_in, w1_in, w2_in,
     third_out, second_out, stat_out, dest, length, tokens, *rest,
 ):
-    r = dict(zip(SCRATCH, rest), fr0=third_out, fr1=second_out)
+    r = dict(zip(SCRATCH, rest))
     sems = rest[len(SCRATCH) :]
     sent = dict(zip(SEMS, sems[0::2]))
     came = dict(zip(SEMS, sems[1::2]))
@@ -585,10 +602,13 @@
             passa_copy(w, k).wait_recv()
             passb_copy(w, k).wait_recv()
 
-    landed(r["send"].at[0:31], came["wave"])
+    loads[4].wait()
+    before_waves(r)
     for k in range(4):
         pass0_copy(k).wait_recv()
-    forward_first(r["got"][...].reshape(512, 128), r["f0"], r)
+    spread_first(r["f0"][...], r)
+    landed(r["send"].at[0:31], came["wave"])
+    forward_first(r["got"][...].reshape(512, 128), r)
     pass_on(0)
     sum_start("t", "g", sum_end("t", "z"))
     gathered(0)
@@ -749,8 +769,7 @@
         for k in (2, 1, 3):
             fx_copy(p, k).start()
 
-    loads[4].wait()
-    third_layer(r["cot"], full[1], r)
+    third_layer(full[1], r)
     core_start(0, grad_third)
     back_second(full[1], r)
     core_end(0)
@@ -773,14 +792,20 @@
     fx_start(0)
     z_end(1, per_token, squares)
     fx_start(1)
+    outs = [(r["fr0"], third_out), (r["fr1"], second_out), (r["stat"], stat_out)]
+    outs = [pltpu.make_async_copy(a, b, came["out"].at[i]) for i, (a, b) in enumerate(outs)]
+    for k in (1, 3, 2):
+        fx_copy(0, k).wait_recv()
+    outs[0].start()
     sum_start("s", "g", sum_end("s", "z"))
+    for k in (1, 3, 2):
+        fx_copy(1, k).wait_recv()
+    outs[1].start()
     rms = jnp.sqrt(sum_end("s", "g") * (1.0 / COUNT))
     factor = (1.0 / (token_sum * jnp.maximum(rms, 1.0)))[0:1, 0:1]
-    stat_out[0:8] = jnp.broadcast_to(factor, (8, 128))
-    stat_out[8:16] = rms
-    for p in range(2):
-        for k in (1, 3, 2):
-            fx_copy(p, k).wait_recv()
+    r["stat"][0:8] = jnp.broadcast_to(factor, (8, 128))
+    r["stat"][8:16] = rms
+    outs[2].start()
 
     landed(r["send"].at[0:31], sent["wave"])
     for k in range(4):
@@ -810,10 +835,11 @@
     for kind in "ts":
         for axis in "zg":
             sum_sent(kind, axis)
+    for copy in outs:
+        copy.wait()
 
 
 def whole(wave, dest, length, tokens, cot, w0, w1, w2):
-    vmem = pl.BlockSpec(memory_space=pltpu.VMEM)
     anywhere = pl.BlockSpec(memory_space=pl.ANY)
     sems = []
     for count in SEMS.values():
@@ -826,7 +852,7 @@
             jax.ShapeDtypeStruct((16, 128), F32),
         ),
         in_specs=[anywhere] * 8,
-        out_specs=(vmem,) * 3,
+        out_specs=(anywhere,) * 3,
         scratch_shapes=[pltpu.SMEM((SEG,), jnp.int32)] * 3
         + [pltpu.VMEM(s, t) for s, t in SCRATCH.values()]
         + sems,
@@ -860,7 +886,7 @@
         ),
         in_specs=[vmem] * 3,
         out_specs=(vmem, vmem, vmem, pl.BlockSpec(memory_space=pltpu.SMEM)),
-        compiler_params=pltpu.CompilerParams(vmem_limit_bytes=16 << 20),
+        compiler_params=pltpu.CompilerParams(vmem_limit_bytes=58 << 20),
     )(third.reshape(64, 3 * D), second.reshape(64, 3 * D + 128), stat)
     return first.T, second, third, rms
 

time: 71.3 us -> 69.4 us (0.973)
  local copies, waits for them, and re-layouts: 2.55 us -> 0 us
    unnamed x6 -> x0, local copies, waits for them, and re-layouts: 2.55 us -> none
    pallas_call x1, Pallas kernels: 0.95 us -> 1.98 us  [local(): pl.pallas_call(scale_kernel, out_shape=(jax.ShapeDtypeStruct((64, 3 * D),...]
where the time goes in v4:
time: 69.4 us; the launch traced here: 68.5 us
  Pallas kernels  67.8 us (98%)
    pallas_call x1, Pallas kernels, whole(): pl.pallas_call(whole_kernel, out_shape=(jax.ShapeDtypeStruct((4, 16, 3 *...  65.8 us
    pallas_call x1, Pallas kernels, local(): pl.pallas_call(scale_kernel, out_shape=(jax.ShapeDtypeStruct((64, 3 * D),...  1.98 us

profile of v4, /device:TPU:1, one launch (start us, length us, event | category | flops | bytes accessed | tf_op | source)
XLA Modules:
  0.0 68.5 jit_solution(10290225577719953961)
XLA Ops:
  0.6 65.8 %shard_map.111 = (bf16[4,16,1536]{2,1,0:T(8,128)(2,1)}, bf16[4,16,1664]{2,1,0:T(8,128)(2,1)}, f32[16,128]{1,0:T(8,128)}) custom-call(f32[8,512]{1,0:T(8,128)} %wave_in.1, s32[8]{0:T(128)} %dest_in.1, s32[8]{0:T(128)} %length_in.1, s32[8]{0:T(128)} %tokens_in.1, bf16[192,512]{1,0:T(8,128)(2,1)} %bitcast.7, bf16[10,64]{1,0:T(8,128)(2,1)} %bitcast.9, ...), custom_call_target="tpu_custom_call" | custom-call | flops 3000000000 | bytes 3000000 | tf_op jit(solution)/shard_map/pallas_call | solution.py:847
  66.5 2.0 %shard_map.112 = (f32[64,1536]{1,0:T(8,128)}, f32[64,1536]{1,0:T(8,128)}, f32[10,64]{1,0:T(8,128)}, f32[1]{0:T(128)}) custom-call(bf16[64,1536]{1,0:T(8,128)(2,1)} %bitcast.6, bf16[64,1664]{1,0:T(8,128)(2,1)} %bitcast.5, f32[16,128]{1,0:T(8,128)} %get-tuple-element.13.stat), custom_call_target="tpu_custom_call" | custom-call | tf_op jit(solution)/shard_map/pallas_call | solution.py:879

commit v5 on v4

--- a/solution.py
+++ b/solution.py
@@ -407,11 +407,12 @@
 }
 SCRATCH["fr0"] = ((4, 16, 3 * D), BF16)
 SCRATCH["fr1"] = ((4, 16, 3 * D + 128), BF16)
-SCRATCH["stat"] = ((16, 128), F32)
+SCRATCH["stat"] = ((8, 128), F32)
 SCRATCH.update(COMPUTE_SCRATCH)
 for kind in ("t", "s"):
     for axis in "zg":
-        SCRATCH["all" + kind + axis] = ((16, 8, 128), F32)
+        if kind + axis != "sg":
+            SCRATCH["all" + kind + axis] = ((16, 8, 128), F32)
         SCRATCH["my" + kind + axis] = ((8, 128), F32)
 
 SEMS = {
@@ -433,13 +434,13 @@
     "fz": 2,
     "fx": 8,
     "sum": 4,
-    "out": 3,
+    "out": 4,
 }
 
 
 def whole_kernel(
     wave_in, dest_in, length_in, tokens_in, cot_in, w0_in, w1_in, w2_in,
-    third_out, second_out, stat_out, dest, length, tokens, *rest,
+    third_out, second_out, squares_out, tokens_out, dest, length, tokens, *rest,
 ):
     r = dict(zip(SCRATCH, rest))
     sems = rest[len(SCRATCH) :]
@@ -494,7 +495,8 @@
 
     def sum_copy(kind, axis, k):
         which = 2 * (kind == "s") + (axis == "g")
-        mine, every = r["my" + kind + axis], r["all" + kind + axis]
+        mine = r["my" + kind + axis]
+        every = squares_out if which == 3 else r["all" + kind + axis]
         if axis == "z":
             me, to = column, column_peer(k)
         else:
@@ -512,7 +514,7 @@
         return jnp.sum(every[...], axis=0)
 
     def sum_sent(kind, axis):
-        every = r["all" + kind + axis]
+        every = r["alltg"]
         landed(every.at[0:15], sent["sum"].at[2 * (kind == "s") + (axis == "g")])
 
     def wave_copy(k):
@@ -792,21 +794,19 @@
     fx_start(0)
     z_end(1, per_token, squares)
     fx_start(1)
-    outs = [(r["fr0"], third_out), (r["fr1"], second_out), (r["stat"], stat_out)]
+    outs = [(r["fr0"], third_out), (r["fr1"], second_out), (r["mysg"], squares_out.at[plane]), (r["stat"], tokens_out)]
     outs = [pltpu.make_async_copy(a, b, came["out"].at[i]) for i, (a, b) in enumerate(outs)]
+    r["stat"][...] = token_sum
+    outs[3].start()
     for k in (1, 3, 2):
         fx_copy(0, k).wait_recv()
     outs[0].start()
-    sum_start("s", "g", sum_end("s", "z"))
+    r["mysg"][...] = sum_end("s", "z")
+    loop(1, 16, lambda k: sum_copy("s", "g", k).start())
+    outs[2].start()
     for k in (1, 3, 2):
         fx_copy(1, k).wait_recv()
     outs[1].start()
-    rms = jnp.sqrt(sum_end("s", "g") * (1.0 / COUNT))
-    factor = (1.0 / (token_sum * jnp.maximum(rms, 1.0)))[0:1, 0:1]
-    r["stat"][0:8] = jnp.broadcast_to(factor, (8, 128))
-    r["stat"][8:16] = rms
-    outs[2].start()
-
     landed(r["send"].at[0:31], sent["wave"])
     for k in range(4):
         pass0_copy(k).wait_send()
@@ -832,11 +832,13 @@
     for p in range(2):
         landed(r["zr" + str(p)].at[0:7], sent["z"].at[p])
         landed(r["fz" + str(p)].at[0:7], sent["fz"].at[p])
-    for kind in "ts":
-        for axis in "zg":
-            sum_sent(kind, axis)
+    sum_sent("t", "z")
+    sum_sent("t", "g")
+    sum_sent("s", "z")
     for copy in outs:
         copy.wait()
+    landed(squares_out.at[0:15], came["sum"].at[3])
+    sum_sent("s", "g")
 
 
 def whole(wave, dest, length, tokens, cot, w0, w1, w2):
@@ -849,10 +851,11 @@
         out_shape=(
             jax.ShapeDtypeStruct((4, 16, 3 * D), BF16),
             jax.ShapeDtypeStruct((4, 16, 3 * D + 128), BF16),
-            jax.ShapeDtypeStruct((16, 128), F32),
+            jax.ShapeDtypeStruct((16, 8, 128), F32),
+            jax.ShapeDtypeStruct((8, 128), F32),
         ),
         in_specs=[anywhere] * 8,
-        out_specs=(anywhere,) * 3,
+        out_specs=(anywhere,) * 4,
         scratch_shapes=[pltpu.SMEM((SEG,), jnp.int32)] * 3
         + [pltpu.VMEM(s, t) for s, t in SCRATCH.values()]
         + sems,
@@ -863,18 +866,19 @@
     )(wave, dest, length, tokens, cot, w0, w1, w2)
 
 
-def scale_kernel(third, second, stat, third_out, second_out, first_out, rms_out):
-    factor = stat[0:1, 0:1]
+def scale_kernel(third, second, squares, tokens, third_out, second_out, first_out, rms_out):
+    rms = jnp.sqrt(jnp.sum(squares[...], axis=0) * (1.0 / COUNT))
+    factor = (1.0 / (tokens[...] * jnp.maximum(rms, 1.0)))[0:1, 0:1]
     third_out[...] = third[...].astype(F32) * factor
     second_out[...] = second[:, 0 : 3 * D].astype(F32) * factor
     first = second[:, 3 * D :].astype(F32) * factor
     square = jnp.concatenate([first, jnp.zeros((64, 128), F32)], axis=0)
     first_out[...] = square.T[0:10, 0:64]
-    rms_out[0] = jnp.max(stat[8:16])
+    rms_out[0] = jnp.max(rms)
 
 
 def local(wave, length, dest, tokens, cot, w0, w1, w2):
-    third, second, stat = whole(wave, dest, length, tokens, cot.reshape(ROWS2, D), w0.T, w1, w2)
+    third, second, squares, total = whole(wave, dest, length, tokens, cot.reshape(ROWS2, D), w0.T, w1, w2)
     vmem = pl.BlockSpec(memory_space=pltpu.VMEM)
     third, second, first, rms = pl.pallas_call(
         scale_kernel,
@@ -884,10 +888,10 @@
             jax.ShapeDtypeStruct((10, 64), F32),
             jax.ShapeDtypeStruct((1,), F32),
         ),
-        in_specs=[vmem] * 3,
+        in_specs=[vmem] * 4,
         out_specs=(vmem, vmem, vmem, pl.BlockSpec(memory_space=pltpu.SMEM)),
         compiler_params=pltpu.CompilerParams(vmem_limit_bytes=58 << 20),
-    )(third.reshape(64, 3 * D), second.reshape(64, 3 * D + 128), stat)
+    )(third.reshape(64, 3 * D), second.reshape(64, 3 * D + 128), squares, total)
     return first.T, second, third, rms
 
 

time: 69.4 us -> 68.9 us (level)
  no operation moved by 1% of the time
where the time goes in v5:
time: 68.9 us; the launch traced here: 68 us
  Pallas kernels  67.4 us (98%)
    pallas_call x1, Pallas kernels, whole(): pl.pallas_call(whole_kernel, out_shape=(jax.ShapeDtypeStruct((4, 16, 3 *...  65.3 us
    pallas_call x1, Pallas kernels, local(): pl.pallas_call(scale_kernel, out_shape=(jax.ShapeDtypeStruct((64, 3 * D),...  2.02 us

profile of v5, /device:TPU:1, one launch (start us, length us, event | category | flops | bytes accessed | tf_op | source)
XLA Modules:
  0.0 68.0 jit_solution(4376895225418893989)
XLA Ops:
  0.6 65.3 %shard_map.111 = (bf16[4,16,1536]{2,1,0:T(8,128)(2,1)}, bf16[4,16,1664]{2,1,0:T(8,128)(2,1)}, f32[16,8,128]{2,1,0:T(8,128)}, f32[8,128]{1,0:T(8,128)}) custom-call(f32[8,512]{1,0:T(8,128)} %wave_in.1, s32[8]{0:T(128)} %dest_in.1, s32[8]{0:T(128)} %length_in.1, s32[8]{0:T(128)} %tokens_in.1, bf16[192,512]{1,0:T(8,128)(2,1)} %bitcast.7, ...), custom_call_target="tpu_custom_call" | custom-call | flops 3000000000 | bytes 3000000 | tf_op jit(solution)/shard_map/pallas_call | solution.py:849
  66.0 2.0 %shard_map.112 = (f32[64,1536]{1,0:T(8,128)}, f32[64,1536]{1,0:T(8,128)}, f32[10,64]{1,0:T(8,128)}, f32[1]{0:T(128)}) custom-call(bf16[64,1536]{1,0:T(8,128)(2,1)} %bitcast.6, bf16[64,1664]{1,0:T(8,128)(2,1)} %bitcast.5, f32[16,8,128]{2,1,0:T(8,128)} %get-tuple-element.14.squares, f32[8,128]{1,0:T(8,128)} %get-tuple-element.15.tokens), custom_call_target="tpu_custom_call" | custom-call | tf_op jit(solution)/shard_map/pallas_call | solution.py:883

commit v6 on v5

--- a/solution.py
+++ b/solution.py
@@ -673,7 +673,7 @@
 
     def fx_copy(p, k):
         here = r["fr" + str(p)].at[x]
-        return remote(here, here, sent["fx"].at[p * 4 + k], came["fx"].at[p * 4 + k], dp, x_peer(k))
+        return remote(here, (third_out, second_out)[p].at[x], sent["fx"].at[p * 4 + k], came["fx"].at[p * 4 + k], dp, x_peer(k))
 
     def core_start(p, grad=None):
         for k in (2, 1, 3, 0):
@@ -793,20 +793,20 @@
     squares = z_end(0, per_token)
     fx_start(0)
     z_end(1, per_token, squares)
-    fx_start(1)
-    outs = [(r["fr0"], third_out), (r["fr1"], second_out), (r["mysg"], squares_out.at[plane]), (r["stat"], tokens_out)]
+    outs = [(r["fr0"].at[x], third_out.at[x]), (r["fr1"].at[x], second_out.at[x]), (r["mysg"], squares_out.at[plane]), (r["stat"], tokens_out)]
     outs = [pltpu.make_async_copy(a, b, came["out"].at[i]) for i, (a, b) in enumerate(outs)]
     r["stat"][...] = token_sum
-    outs[3].start()
-    for k in (1, 3, 2):
-        fx_copy(0, k).wait_recv()
-    outs[0].start()
     r["mysg"][...] = sum_end("s", "z")
     loop(1, 16, lambda k: sum_copy("s", "g", k).start())
     outs[2].start()
-    for k in (1, 3, 2):
-        fx_copy(1, k).wait_recv()
+    fx_start(1)
     outs[1].start()
+    outs[0].start()
+    r["stat"][...] = token_sum
+    outs[3].start()
+    for p in range(2):
+        for k in (1, 3, 2):
+            fx_copy(p, k).wait_recv()
     landed(r["send"].at[0:31], sent["wave"])
     for k in range(4):
         pass0_copy(k).wait_send()

time: 68.9 us -> 69.7 us (1.012); the launches traced: 68 us -> 69.6 us
  Pallas kernels: 67.4 us -> 69 us
    pallas_call x1, Pallas kernels: 65.3 us -> 67 us  [whole(): pl.pallas_call(whole_kernel, out_shape=(jax.ShapeDtypeStruct((4, 16, 3 *...]
where the time goes in v6:
time: 69.7 us; the launch traced here: 69.6 us
  Pallas kernels  69 us (99%)
    pallas_call x1, Pallas kernels, whole(): pl.pallas_call(whole_kernel, out_shape=(jax.ShapeDtypeStruct((4, 16, 3 *...  67 us
    pallas_call x1, Pallas kernels, local(): pl.pallas_call(scale_kernel, out_shape=(jax.ShapeDtypeStruct((64, 3 * D),...  2.02 us

profile of v6, /device:TPU:1, one launch (start us, length us, event | category | flops | bytes accessed | tf_op | source)
XLA Modules:
  0.0 69.6 jit_solution(12166781692918929886)
XLA Ops:
  0.6 67.0 %shard_map.111 = (bf16[4,16,1536]{2,1,0:T(8,128)(2,1)}, bf16[4,16,1664]{2,1,0:T(8,128)(2,1)}, f32[16,8,128]{2,1,0:T(8,128)}, f32[8,128]{1,0:T(8,128)}) custom-call(f32[8,512]{1,0:T(8,128)} %wave_in.1, s32[8]{0:T(128)} %dest_in.1, s32[8]{0:T(128)} %length_in.1, s32[8]{0:T(128)} %tokens_in.1, bf16[192,512]{1,0:T(8,128)(2,1)} %bitcast.7, ...), custom_call_target="tpu_custom_call" | custom-call | flops 3000000000 | bytes 3000000 | tf_op jit(solution)/shard_map/pallas_call | solution.py:849
  67.6 2.0 %shard_map.112 = (f32[64,1536]{1,0:T(8,128)}, f32[64,1536]{1,0:T(8,128)}, f32[10,64]{1,0:T(8,128)}, f32[1]{0:T(128)}) custom-call(bf16[64,1536]{1,0:T(8,128)(2,1)} %bitcast.6, bf16[64,1664]{1,0:T(8,128)(2,1)} %bitcast.5, f32[16,8,128]{2,1,0:T(8,128)} %get-tuple-element.14.squares, f32[8,128]{1,0:T(8,128)} %get-tuple-element.15.tokens), custom_call_target="tpu_custom_call" | custom-call | tf_op jit(solution)/shard_map/pallas_call | solution.py:883
